TPU v7x, 32 devices: a whole 2x2x4 slice. The times are simulated.
32 devices in a mesh: batch: 16 (over z, y, x), tower: 2 (over core).
Axes of the slice: x: 2, y: 2, z: 4, core: 2. Of those that a mesh axis runs over, the one named last changes fastest.
Arguments:
- crop_maps: bfloat16 [512, 2, 13, 13, 384], P(('batch', 'tower')), may hold values from -6 to 6
- cotangent: bfloat16 [512, 2, 4096], P('batch', None, 'tower'), may hold values from -48 to 48
- crop_counts: int32 [256], P('batch'), may hold values from 1 to 2, as said below
- filter_weight: float32 [6912, 256], P(('batch', 'tower')), may hold values from -0.109375 to 0.109375
- filter_first: float32 [6912, 256], P(('batch', 'tower')), may hold values from -640 to 640
- filter_second: float32 [6912, 256], P(('batch', 'tower')), may hold values from 13652.503 to 54610.01
- conv_filter_bias: float32 [512], P(('batch', 'tower')), may hold values from -0.625 to 0.625
- conv_filter_bias_mean: float32 [512], P(('batch', 'tower')), may hold values from -640 to 640
- conv_filter_bias_variance: float32 [512], P(('batch', 'tower')), may hold values from 13652.503 to 54610.01
- pool_stitch: float32 [1024], P(('batch', 'tower')), may hold values from 0.15 to 1
- pool_stitch_first: float32 [1024], P(('batch', 'tower')), may hold values from -1280 to 1280
- pool_stitch_second: float32 [1024], P(('batch', 'tower')), may hold values from 55296 to 221184
- dense_weight: float32 [2, 9216, 4096], P('tower', 'batch'), may hold values from -0.125 to 0.125
- dense_weight_first: float32 [2, 9216, 4096], P('tower', 'batch'), may hold values from -160 to 160
- dense_weight_second: float32 [2, 9216, 4096], P('tower', 'batch'), may hold values from 864 to 3456
- dense_bias: float32 [2, 4096], P('tower'), may hold values from -0.625 to 0.625
- dense_bias_first: float32 [2, 4096], P('tower'), may hold values from -512 to 512
- dense_bias_second: float32 [2, 4096], P('tower'), may hold values from 7104 to 28416
- dense_stitch: float32 [2, 2, 4096], P(None, None, 'tower'), may hold values from 0.15 to 1
- dense_stitch_first: float32 [2, 2, 4096], P(None, None, 'tower'), may hold values from -448 to 448
- dense_stitch_second: float32 [2, 2, 4096], P(None, None, 'tower'), may hold values from 4992 to 19968
Outputs:
- stitched: bfloat16 [512, 2, 4096], P('batch', None, 'tower')
- input_grad: bfloat16 [512, 2, 13, 13, 384], P(('batch', 'tower'))
- new_filter_weight: float32 [6912, 256], P(('batch', 'tower'))
- new_filter_first: float32 [6912, 256], P(('batch', 'tower'))
- new_filter_second: float32 [6912, 256], P(('batch', 'tower'))
- filter_copy: bfloat16 [6912, 256], P(('batch', 'tower'))
- new_filter_bias: float32 [512], P(('batch', 'tower'))
- new_filter_bias_first: float32 [512], P(('batch', 'tower'))
- new_filter_bias_second: float32 [512], P(('batch', 'tower'))
- new_pool_stitch: float32 [1024], P(('batch', 'tower'))
- new_pool_stitch_first: float32 [1024], P(('batch', 'tower'))
- new_pool_stitch_second: float32 [1024], P(('batch', 'tower'))
- new_dense_weight: float32 [2, 9216, 4096], P('tower', 'batch')
- new_dense_first: float32 [2, 9216, 4096], P('tower', 'batch')
- new_dense_second: float32 [2, 9216, 4096], P('tower', 'batch')
- dense_copy: bfloat16 [2, 9216, 4096], P('tower', 'batch')
- new_dense_bias: float32 [2, 4096], P('tower')
- new_dense_bias_first: float32 [2, 4096], P('tower')
- new_dense_bias_second: float32 [2, 4096], P('tower')
- new_dense_stitch: float32 [2, 2, 4096], P(None, None, 'tower')
- new_dense_stitch_first: float32 [2, 2, 4096], P(None, None, 'tower')
- new_dense_stitch_second: float32 [2, 2, 4096], P(None, None, 'tower')
Inputs may be any that keep to these rules, and one draw needn't show every extreme that they name: `crop_counts`: block b of 16 crop slots holds the crops of images b * 8 to b * 8 + 7 in order, then empty slots; in every draw some block is full.
All inputs are finite; a program needn't handle non-finite values.
Results may differ from a plain program's by a relative error of at most 0.0093.
Values may be sent and summed in bfloat16 or wider, within the bound.
No kernel may reach another device: no remote copies, remote signals or barrier semaphores. Data moves between devices by JAX's collectives and lax.ppermute only.
A program may use at most 448 MiB of HBM per device.

v0:
```python
import functools

import jax
import jax.numpy as jnp
from jax import lax
from jax.experimental import pallas as pl
from jax.experimental.pallas import tpu as pltpu
from jax.sharding import PartitionSpec as P

STEP = 10


BETA_ONE = 0.5
BETA_TWO = 0.5
EPSILON = 1e-08
DECAY = 0.01
RATE_FILTER = 0.02
RATE_DENSE = 0.02
BIAS_LEARN_RATE = 0.05
RATE_STITCH = 0.2


def smooth_gate(values):
    return jax.nn.gelu(values, approximate=True)


def gate_slope(values):
    return jax.vjp(smooth_gate, values)[1](jnp.ones_like(values))[0]


def pool_mean(active):
    pooled_side = (active.shape[1] - 1) // 2
    span = 2 * pooled_side - 1
    total = jnp.zeros((), jnp.float32)
    for row_start in range(3):
        for col_start in range(3):
            total = total + active[:, row_start : row_start + span : 2, col_start : col_start + span : 2]
    return total / 9.0


def pool_spread(gradient, full_side):
    scaled = gradient / 9.0
    for axis in (1, 2):
        even = jnp.concatenate([scaled, jnp.zeros_like(lax.slice_in_dim(scaled, 0, 1, axis=axis))], axis)
        shifted = jnp.concatenate([jnp.zeros_like(lax.slice_in_dim(scaled, 0, 1, axis=axis)), scaled], axis)
        pairs = jnp.stack([even + shifted, even], axis + 1)
        shape = list(scaled.shape)
        shape[axis] = 2 * shape[axis] + 2
        scaled = lax.slice_in_dim(pairs.reshape(shape), 0, full_side, axis=axis)
    return scaled


def decoupled_adam_step(master, first, second, grad, rate, decay):
    first_new = BETA_ONE * first + (1.0 - BETA_ONE) * grad
    second_new = BETA_TWO * second + (1.0 - BETA_TWO) * grad * grad
    first_hat = first_new / (1.0 - BETA_ONE**STEP)
    second_hat = second_new / (1.0 - BETA_TWO**STEP)
    master_new = master - rate * (first_hat / (jnp.sqrt(second_hat) + EPSILON) + decay * master)
    return (master_new, first_new, second_new)


def core_swap(values):
    return lax.ppermute(values, "tower", [(0, 1), (1, 0)])


def by_core(core, own, other):
    return jnp.where(
        core == 0,
        jnp.concatenate([own, other], axis=-1),
        jnp.concatenate([other, own], axis=-1),
    )


def gradients_any(
    crop_maps,
    cotangent,
    crop_counts,
    filter_weight,
    conv_filter_bias,
    pool_stitch,
    dense_weight,
    dense_weight_first,
    dense_weight_second,
    dense_bias,
    dense_stitch,
):
    block_rows = crop_maps.shape[0]
    side = crop_maps.shape[2]
    in_width = crop_maps.shape[4]
    filter_rows, out_width = filter_weight.shape
    chips = lax.axis_size("batch")
    chip = lax.axis_index("batch")
    core = lax.axis_index("tower")
    totals = jnp.sum(crop_counts.reshape(2, -1), axis=1)
    slots = jnp.arange(block_rows, dtype=jnp.int32)
    mask = (slots[None, :] < totals[:, None]).astype(jnp.float32).reshape(-1)
    pair_rows = 2 * block_rows
    dense_rows, unit_width = dense_weight.shape[1:]
    half_width = unit_width // 2
    bias_width = conv_filter_bias.shape[0]
    small_width = bias_width + pool_stitch.shape[0]
    pack_rows = -(-(filter_rows + 1) // 16) * 16
    small = jnp.concatenate([conv_filter_bias, pool_stitch])
    small = jnp.pad(small, (0, (pack_rows - filter_rows) * out_width - small_width))
    packed = jnp.concatenate([filter_weight, small.reshape(-1, out_width)]).astype(jnp.bfloat16)
    gathered = lax.all_gather(packed, ("batch", "tower"), axis=0)
    filters = gathered[:, :filter_rows].reshape(2, 3, 3, in_width, out_width)
    small_full = gathered[:, filter_rows, :small_width].astype(jnp.float32)
    biases = small_full[:, :bias_width].reshape(2, out_width)
    pool_low = small_full[:, bias_width:].reshape(2, 2, out_width)
    maps = jnp.transpose(crop_maps, (1, 2, 3, 0, 4))
    grad_out = cotangent.astype(jnp.float32) * mask[:, None, None]
    own_stitch = lax.dynamic_index_in_dim(dense_stitch, core, axis=1, keepdims=False)
    other_stitch = lax.dynamic_index_in_dim(dense_stitch, 1 - core, axis=1, keepdims=False)
    own_grad = jnp.sum(own_stitch * grad_out, axis=1).astype(jnp.bfloat16)
    other_grad = core_swap(jnp.sum(other_stitch * grad_out, axis=1).astype(jnp.bfloat16))
    grad_active = by_core(core, own_grad, other_grad)
    dense_low = dense_weight[0].astype(jnp.bfloat16)
    conv = jnp.stack(
        [
            lax.conv_general_dilated(
                maps[tower],
                filters[tower],
                (1, 1),
                ((1, 1), (1, 1)),
                dimension_numbers=("HWNC", "HWIO", "HWNC"),
                preferred_element_type=jnp.float32,
            )
            for tower in range(2)
        ]
    )
    conv = conv + biases[:, None, None, None, :]
    pooled = pool_mean(smooth_gate(conv))
    pooled_side = pooled.shape[1]
    mixed = jnp.sum(pool_low[:, :, None, None, None, :] * pooled[None], axis=1).astype(jnp.bfloat16)
    mixed = jnp.transpose(mixed, (0, 3, 1, 2, 4)).reshape(2, block_rows, chips, dense_rows)
    mixed = jnp.transpose(mixed, (0, 2, 1, 3))
    own_mixed = lax.dynamic_index_in_dim(mixed, core, axis=0, keepdims=False)
    other_mixed = core_swap(lax.dynamic_index_in_dim(mixed, 1 - core, axis=0, keepdims=False))
    features = jnp.where(
        core == 0,
        jnp.concatenate([own_mixed, other_mixed], axis=1),
        jnp.concatenate([other_mixed, own_mixed], axis=1),
    )
    columns = lax.all_to_all(features, "batch", split_axis=0, concat_axis=0, tiled=True)
    columns = columns.reshape(-1, dense_rows)
    partial = jnp.dot(columns, dense_low, preferred_element_type=jnp.float32)
    hidden = lax.psum_scatter(partial, "batch", scatter_dimension=0, tiled=True) + dense_bias
    grad_hidden = (grad_active.astype(jnp.float32) * gate_slope(hidden)).astype(jnp.bfloat16)
    grad_full = lax.all_gather(grad_hidden, "batch", axis=0, tiled=True)
    active = smooth_gate(hidden).astype(jnp.bfloat16)
    own_active = lax.dynamic_slice_in_dim(active, core * half_width, half_width, axis=1)
    other_active = core_swap(
        lax.dynamic_slice_in_dim(active, (1 - core) * half_width, half_width, axis=1)
    )
    own_active = own_active.astype(jnp.float32)[:, None]
    other_active = other_active.astype(jnp.float32)[:, None]
    stitched = own_stitch * own_active + other_stitch * other_active
    stitched = (stitched * mask[:, None, None]).astype(jnp.bfloat16)
    grad_own_stitch = jnp.sum(grad_out * own_active, axis=0)
    grad_other_stitch = jnp.sum(grad_out * other_active, axis=0)
    grad_dense_stitch = lax.psum(
        jnp.where(
            core == 0,
            jnp.stack([grad_own_stitch, grad_other_stitch], axis=1),
            jnp.stack([grad_other_stitch, grad_own_stitch], axis=1),
        ),
        "batch",
    )
    grad_columns = lax.dot_general(
        grad_full, dense_low, (((1,), (1,)), ((), ())), preferred_element_type=jnp.float32
    ).astype(jnp.bfloat16)
    grad_columns = grad_columns.reshape(chips, pair_rows, dense_rows)
    returned = lax.all_to_all(grad_columns, "batch", split_axis=0, concat_axis=0, tiled=True)
    grad_dense_bias = jnp.sum(grad_full.astype(jnp.float32), axis=0)
    grad_dense_weight = lax.dot_general(
        columns, grad_full, (((0,), (0,)), ((), ())), preferred_element_type=jnp.float32
    )
    halves = returned.reshape(chips, 2, block_rows, dense_rows)
    own_mixed = lax.dynamic_index_in_dim(halves, core, axis=1, keepdims=False)
    other_mixed = core_swap(lax.dynamic_index_in_dim(halves, 1 - core, axis=1, keepdims=False))
    grad_mixed = jnp.where(
        core == 0, jnp.stack([own_mixed, other_mixed]), jnp.stack([other_mixed, own_mixed])
    )
    grad_mixed = jnp.transpose(grad_mixed, (0, 2, 1, 3)).reshape(
        2, block_rows, pooled_side, pooled_side, out_width
    )
    grad_mixed = jnp.transpose(grad_mixed, (0, 2, 3, 1, 4)).astype(jnp.float32)
    grad_pool_stitch = jnp.sum(grad_mixed[:, None] * pooled[None], axis=(2, 3, 4))
    grad_pooled = jnp.sum(pool_low[:, :, None, None, None, :] * grad_mixed[:, None], axis=0)
    grad_conv = (pool_spread(grad_pooled, side) * gate_slope(conv)).astype(jnp.bfloat16)
    grad_filter_bias = jnp.sum(grad_conv.astype(jnp.float32), axis=(1, 2, 3))
    weight_dims = lax.ConvDimensionNumbers((3, 2, 0, 1), (3, 2, 0, 1), (2, 3, 0, 1))
    grad_filter_weight = jnp.stack(
        [
            lax.conv_general_dilated(
                maps[tower],
                grad_conv[tower],
                (1, 1),
                ((1, 1), (1, 1)),
                dimension_numbers=weight_dims,
                preferred_element_type=jnp.float32,
            )
            for tower in range(2)
        ]
    )
    filter_sums = lax.psum_scatter(
        grad_filter_weight.reshape(-1, out_width),
        ("batch", "tower"),
        scatter_dimension=0,
        tiled=True,
    )
    small_grad = jnp.concatenate(
        [grad_filter_bias.reshape(2 * chips, -1), grad_pool_stitch.reshape(2 * chips, -1)], axis=1
    )
    small_grad = lax.psum(small_grad, ("batch", "tower"))
    small_grad = lax.dynamic_index_in_dim(small_grad, chip * 2 + core, axis=0, keepdims=False)
    filter_bias_sums = small_grad[:bias_width]
    pool_sums = small_grad[bias_width:]
    input_grad = jnp.stack(
        [
            lax.conv_general_dilated(
                grad_conv[tower],
                filters[tower][::-1, ::-1],
                (1, 1),
                ((1, 1), (1, 1)),
                dimension_numbers=("HWNC", "HWOI", "HWNC"),
                preferred_element_type=jnp.float32,
            ).astype(jnp.bfloat16)
            for tower in range(2)
        ]
    )
    input_grad = jnp.transpose(input_grad, (3, 0, 1, 2, 4))
    update = decoupled_adam_step(
        dense_weight, dense_weight_first, dense_weight_second, grad_dense_weight[None], RATE_DENSE, DECAY
    )
    return (
        stitched,
        input_grad,
        filter_sums,
        filter_bias_sums,
        pool_sums,
        (*update, update[0].astype(jnp.bfloat16)),
        grad_dense_bias,
        grad_dense_stitch,
    )


CUBE = 16
LANES = 128
VMEM_ASKED = 8 << 20
GELU_SCALE = 0.7978845608028654
GELU_CUBIC = 0.044715


def hop(values, level):
    return lax.ppermute(values, "batch", [(i, i ^ (4 * level)) for i in range(CUBE)])


def plane_hop(values, offset):
    return lax.ppermute(values, "batch", [(i, i ^ offset) for i in range(CUBE)])


SIDES = ((0, 1, 2, 3), (0, 2, 1, 3))


def zero_of(values):
    first = values[(0,) * values.ndim]
    return (first != first).astype(jnp.int32)


def held(values, *others):
    zero = sum(zero_of(other) for other in others)
    return jnp.where(zero == 0, values, jnp.zeros((), values.dtype))


def gather_levels(block):
    return [hop(block, level) if level else block for level in range(4)]


def gather_plane(tops, *others):
    groups, halves = [], []
    for group in range(2):
        own = jnp.stack(tops[2 * group : 2 * group + 2])
        if group and others:
            own = held(own, *others)
        half = jnp.stack([own, plane_hop(own, SIDES[group][1])])
        halves.append(half)
        groups.append(jnp.concatenate([half, plane_hop(half, SIDES[group][2])]))
    return groups, halves


def reduce_first(parts, group):
    sent = plane_hop(parts[2:], SIDES[group][2])
    return parts[:2].astype(jnp.float32) + sent.astype(jnp.float32)


def reduce_second(kept, group):
    sent = plane_hop(kept[1].astype(jnp.bfloat16), SIDES[group][1])
    return kept[0] + sent.astype(jnp.float32)


def reduce_levels(groups):
    total = groups[0][0]
    for level in (1, 2, 3):
        part = hop(groups[level // 2][level % 2].astype(jnp.bfloat16), level)
        total = total + part.astype(jnp.float32)
    return total


def on_chip():
    return pl.BlockSpec(memory_space=pltpu.VMEM)


def turn(values):
    return pltpu.roll(values, LANES // 2, axis=1)


def mix_kernel(
    maps_a,
    maps_b,
    small,
    slope_a,
    slope_b,
    pooled,
    sent,
    row_sums,
    means,
):
    side, width, crops, channels = maps_a.shape
    count = (width - 1) // 2

    def gate_row(y, carry):
        for tower, (maps, slopes) in enumerate(((maps_a, slope_a), (maps_b, slope_b))):
            bias = small[tower][None]
            running = [None] * count
            for x in range(width):
                value = maps[y, x] + bias
                square = value * value
                bend = jnp.tanh(GELU_SCALE * value * (1.0 + GELU_CUBIC * square))
                half = 0.5 + 0.5 * bend
                rise = GELU_SCALE * (1.0 + 3.0 * GELU_CUBIC * square)
                slope = half + 0.5 * value * (1.0 - bend * bend) * rise
                slopes[y, x] = slope.astype(jnp.bfloat16)
                gate = value * half
                for place_x in range(max(0, (x - 1) // 2), min(count - 1, x // 2) + 1):
                    old = running[place_x]
                    running[place_x] = gate if old is None else old + gate
            for place_x in range(count):
                row_sums[tower, y, place_x] = running[place_x]
        return carry

    lax.fori_loop(0, side, gate_row, 0)

    def mean_row(row, carry):
        for tower in range(2):
            for place_x in range(count):
                mean = (
                    row_sums[tower, 2 * row, place_x]
                    + row_sums[tower, 2 * row + 1, place_x]
                    + row_sums[tower, 2 * row + 2, place_x]
                ) * (1.0 / 9.0)
                means[tower, row * count + place_x] = mean
                pooled[tower, row * count + place_x] = mean.astype(jnp.bfloat16)
        return carry

    lax.fori_loop(0, count, mean_row, 0)
    low_lanes = lax.broadcasted_iota(jnp.int32, (crops, LANES), 1) < LANES // 2
    halves = small.shape[1] // LANES
    for pair in range(CUBE // 2):
        for tower in range(2):
            tiles = []
            for tile in range(9 * pair, 9 * pair + 9):
                cell, first = tile // halves, tile % halves * LANES
                lanes = slice(first, first + LANES)
                tiles.append(
                    small[2 + 2 * tower, lanes][None] * means[0, cell, :, lanes]
                    + small[3 + 2 * tower, lanes][None] * means[1, cell, :, lanes]
                )
            turned = [turn(tile) for tile in tiles[4:]]
            blank = jnp.zeros_like(tiles[0])
            even = tiles[:4] + [jnp.where(low_lanes, tiles[4], blank)]
            odd = [jnp.where(low_lanes, turned[q], turned[q + 1]) for q in range(4)]
            odd.append(jnp.where(low_lanes, turned[4], blank))
            for chunk, pieces in ((2 * pair, even), (2 * pair + 1, odd)):
                for q, piece in enumerate(pieces):
                    lanes = slice(q * LANES, (q + 1) * LANES)
                    sent[2 * chunk + tower, :, lanes] = piece.astype(jnp.bfloat16)


def mix(conv, small, wide):
    side, _, crops, width = conv[0].shape
    count = (side - 1) // 2
    cells = count * count
    slope = jax.ShapeDtypeStruct(conv[0].shape, jnp.bfloat16)
    pooled = jax.ShapeDtypeStruct((2, cells, crops, width), jnp.bfloat16)
    sent = jax.ShapeDtypeStruct((2 * CUBE, crops, wide), jnp.bfloat16)
    return pl.pallas_call(
        mix_kernel,
        out_shape=(slope, slope, pooled, sent),
        in_specs=[on_chip()] * 3,
        out_specs=(on_chip(),) * 4,
        scratch_shapes=[
            pltpu.VMEM((2, side, count, crops, width), jnp.float32),
            pltpu.VMEM((2, cells, crops, width), jnp.float32),
        ],
        compiler_params=pltpu.CompilerParams(vmem_limit_bytes=VMEM_ASKED),
        cost_estimate=pl.CostEstimate(
            flops=60 * conv[0].size,
            bytes_accessed=12 * conv[0].size,
            transcendentals=2 * conv[0].size,
        ),
        name="gate_pool_mix",
    )(conv[0], conv[1], small)


def back_kernel(
    returned,
    pooled,
    small,
    slope_a,
    slope_b,
    grad_a,
    grad_b,
    grad_small,
    mixed,
    spread,
):
    side, width, crops, channels = slope_a.shape
    count = (width - 1) // 2
    halves = channels // LANES
    low_lanes = lax.broadcasted_iota(jnp.int32, (crops, LANES), 1) < LANES // 2
    for pair in range(CUBE // 2):
        for tower in range(2):
            loaded = []
            for chunk in (2 * pair, 2 * pair + 1):
                source = 2 * chunk + tower
                pieces = []
                for q in range(5):
                    lanes = slice(q * LANES, (q + 1) * LANES)
                    pieces.append(returned[source, :, lanes].astype(jnp.float32))
                loaded.append(pieces)
            even, odd = loaded
            turned = [turn(tile) for tile in odd]
            tiles = even[:4] + [jnp.where(low_lanes, even[4], turned[0])]
            tiles += [jnp.where(low_lanes, turned[q], turned[q + 1]) for q in range(4)]
            for q, tile in enumerate(tiles):
                first = (9 * pair + q) % halves * LANES
                mixed[tower, (9 * pair + q) // halves, :, first : first + LANES] = tile
    blank = jnp.zeros((crops, channels), jnp.float32)
    for tower in range(2):
        for place_x in range(count):
            spread[tower, 0, place_x] = blank
            spread[tower, count + 1, place_x] = blank

    def unmix(row, totals):
        totals = list(totals)
        for place_x in range(count):
            cell = row * count + place_x
            grads = [mixed[tower, cell] for tower in range(2)]
            values = [pooled[tower, cell].astype(jnp.float32) for tower in range(2)]
            for i in range(2):
                for j in range(2):
                    totals[2 * i + j] = totals[2 * i + j] + grads[i] * values[j]
            for j in range(2):
                spread[j, row + 1, place_x] = (
                    small[2 + j][None] * grads[0] + small[4 + j][None] * grads[1]
                ) * (1.0 / 9.0)
        return tuple(totals)

    totals = lax.fori_loop(0, count, unmix, (blank,) * 4)
    for which in range(4):
        grad_small[2 + which] = jnp.sum(totals[which], axis=0)

    def spread_row(y, totals):
        totals = list(totals)
        row = y // 2
        both = (1 - y % 2).astype(jnp.float32)
        for tower, (slopes, grads) in enumerate(((slope_a, grad_a), (slope_b, grad_b))):
            line = [
                spread[tower, row + 1, place_x] + both * spread[tower, row, place_x]
                for place_x in range(count)
            ]
            for x in range(width):
                near = [line[q] for q in range(max(0, (x - 1) // 2), min(count - 1, x // 2) + 1)]
                value = near[0] if len(near) == 1 else near[0] + near[1]
                value = (value * slopes[y, x].astype(jnp.float32)).astype(jnp.bfloat16)
                grads[y, x] = value
                totals[tower] = totals[tower] + value.astype(jnp.float32)
        return tuple(totals)

    totals = lax.fori_loop(0, side, spread_row, (blank,) * 2)
    for tower in range(2):
        grad_small[tower] = jnp.sum(totals[tower], axis=0)


def back(returned, pooled, small, slopes):
    side, _, crops, width = slopes[0].shape
    count = (side - 1) // 2
    grad = jax.ShapeDtypeStruct(slopes[0].shape, jnp.bfloat16)
    return pl.pallas_call(
        back_kernel,
        out_shape=(grad, grad, jax.ShapeDtypeStruct((6, width), jnp.float32)),
        in_specs=[on_chip()] * 5,
        out_specs=(on_chip(),) * 3,
        scratch_shapes=[
            pltpu.VMEM((2, count * count, crops, width), jnp.float32),
            pltpu.VMEM((2, count + 2, count, crops, width), jnp.float32),
        ],
        compiler_params=pltpu.CompilerParams(vmem_limit_bytes=VMEM_ASKED),
        cost_estimate=pl.CostEstimate(
            flops=20 * slopes[0].size, bytes_accessed=8 * slopes[0].size, transcendentals=0
        ),
        name="pool_gradient",
    )(returned, pooled, small, slopes[0], slopes[1])


def order_kernel(place, *refs):
    back = len(refs) == 4
    blocks, groups = (refs[3], refs[:2]) if back else (refs[0], refs[1:])
    chip = 4 * place[0] + place[1]
    rows = blocks.shape[1]
    last = blocks.shape[2] - LANES
    for group in range(2):
        for side in range(4):
            for level in range(2):
                at = chip ^ (4 * (2 * group + level) + SIDES[group][side])
                start = (2 * side + level) * rows
                if back:
                    half = rows // 2
                    for first in (start, start + half):
                        into = pl.ds(first - start, half)
                        blocks[at, into, :last] = groups[group][first : first + half, :last]
                        blocks[at, into, last:] = groups[group][first : first + half, last:] + refs[2][...]
                else:
                    groups[group][start : start + rows] = blocks[at]


def order_rows(place, *arrays):
    if len(arrays) == 1:
        _, rows, width = arrays[0].shape
        outs = [jax.ShapeDtypeStruct((CUBE // 2 * rows, width), arrays[0].dtype)] * 2
    else:
        rows, width = arrays[0].shape
        outs = jax.ShapeDtypeStruct((CUBE, rows // (CUBE // 2), width), arrays[0].dtype)
    size = arrays[0].size * (1 if len(arrays) == 1 else 2)
    return pl.pallas_call(
        order_kernel,
        out_shape=outs,
        in_specs=[pl.BlockSpec(memory_space=pltpu.SMEM)] + [on_chip()] * len(arrays),
        out_specs=[on_chip()] * 2 if len(arrays) == 1 else on_chip(),
        compiler_params=pltpu.CompilerParams(vmem_limit_bytes=VMEM_ASKED),
        cost_estimate=pl.CostEstimate(flops=size, bytes_accessed=4 * size, transcendentals=0),
        name="order_rows",
    )(place, *arrays)


def pair_kernel(place, own, other, blocks_a, blocks_b):
    chip = 4 * place[0] + place[1]
    for group, blocks in enumerate((blocks_a, blocks_b)):
        for side in range(4):
            for level in range(2):
                source = chip ^ (4 * (2 * group + level) + SIDES[group][side])
                total = own[source].astype(jnp.float32) + other[source].astype(jnp.float32)
                blocks[side, level] = total.astype(jnp.bfloat16)


def pair_blocks(place, own, other):
    blocks = jax.ShapeDtypeStruct((4, 2) + own.shape[1:], own.dtype)
    return pl.pallas_call(
        pair_kernel,
        out_shape=(blocks, blocks),
        in_specs=[pl.BlockSpec(memory_space=pltpu.SMEM), on_chip(), on_chip()],
        out_specs=(on_chip(), on_chip()),
        compiler_params=pltpu.CompilerParams(vmem_limit_bytes=VMEM_ASKED),
        cost_estimate=pl.CostEstimate(
            flops=own.size, bytes_accessed=6 * own.size, transcendentals=0
        ),
        name="pair_blocks",
    )(place, own, other)


def dense_kernel(order, columns, grads_a, grads_b, weight, first, second, *outs):
    new_weight, new_first, new_second, copy, grad_bias = outs[-5:]
    rows = grads_a.shape[0]
    grad = jnp.dot(columns[:, :rows], grads_a[...], preferred_element_type=jnp.float32)
    grad += jnp.dot(columns[:, rows:], grads_b[...], preferred_element_type=jnp.float32)
    updated, mean, square = decoupled_adam_step(
        weight[0], first[0], second[0], grad[: weight.shape[1]], RATE_DENSE, DECAY
    )
    new_weight[0] = updated
    new_first[0] = mean
    new_second[0] = square
    copy[0] = updated.astype(jnp.bfloat16)
    grad_bias[...] = jnp.sum(
        grads_a[...].astype(jnp.float32) + grads_b[...].astype(jnp.float32), axis=0, keepdims=True
    )


def dense_update(order, columns, grads, weight, first, second, part, parts, old):
    tile = 1024
    _, rows, units = weight.shape
    steps = units // tile // parts
    state = pl.BlockSpec((1, rows, tile), lambda step: (0, 0, part * steps + step))
    grad = pl.BlockSpec((grads[0].shape[0], tile), lambda step: (0, step))
    outs = [jax.ShapeDtypeStruct(weight.shape, jnp.float32)] * 3
    outs += [
        jax.ShapeDtypeStruct(weight.shape, jnp.bfloat16),
        jax.ShapeDtypeStruct((1, units), jnp.float32),
    ]
    return pl.pallas_call(
        dense_kernel,
        grid=(steps,),
        out_shape=outs,
        in_specs=[
            pl.BlockSpec(memory_space=pltpu.SMEM),
            pl.BlockSpec(columns.shape, lambda step: (0, 0)),
            grad,
            grad,
            state,
            state,
            state,
            *[pl.BlockSpec(memory_space=pl.ANY)] * len(old),
        ],
        out_specs=[state] * 4 + [pl.BlockSpec((1, tile), lambda step: (0, part * steps + step))],
        input_output_aliases={7 + i: i for i in range(len(old))},
        compiler_params=pltpu.CompilerParams(vmem_limit_bytes=48 << 20),
        cost_estimate=pl.CostEstimate(
            flops=2 * columns.size * units // parts,
            bytes_accessed=26 * weight.size // parts,
            transcendentals=weight.size // parts,
        ),
        name="dense_update",
    )(order, columns, *grads, weight, first, second, *old)


def gradients_cube(
    crop_maps,
    cotangent,
    crop_counts,
    filter_weight,
    conv_filter_bias,
    pool_stitch,
    dense_weight,
    dense_weight_first,
    dense_weight_second,
    dense_bias,
    dense_stitch,
):
    crops = crop_maps.shape[0]
    in_width = crop_maps.shape[4]
    filter_rows, out_width = filter_weight.shape
    chip, core = lax.axis_index("batch"), lax.axis_index("tower")
    own_level, own_plane = chip // 4, chip % 4
    place = jnp.stack([own_level, own_plane, core]).astype(jnp.int32)
    totals = jnp.sum(crop_counts.reshape(2, -1), axis=1)
    slots = jnp.arange(crops, dtype=jnp.int32)
    mask = (slots[None, :] < totals[:, None]).astype(jnp.float32).reshape(-1)
    rows = 2 * crops
    dense_rows, unit_width = dense_weight.shape[1:]
    half_width = unit_width // 2
    wide = -(-dense_rows // LANES) * LANES
    bias_width = conv_filter_bias.shape[0]
    small_width = bias_width + pool_stitch.shape[0]
    pack_rows = -(-(filter_rows + 1) // 16) * 16
    small = jnp.concatenate([conv_filter_bias, pool_stitch])
    small = jnp.pad(small, (0, (pack_rows - filter_rows) * out_width - small_width))
    packed = jnp.concatenate([filter_weight, small.reshape(-1, out_width)]).astype(jnp.bfloat16)
    maps = jnp.transpose(crop_maps, (1, 2, 3, 0, 4))
    tops = gather_levels(packed)
    own_packed = jnp.zeros((CUBE,) + packed.shape, packed.dtype)
    for group, blocks in enumerate(gather_plane(tops)[0]):
        for side in range(4):
            for level in range(2):
                owner = chip ^ (4 * (2 * group + level) + SIDES[group][side])
                own_packed = lax.dynamic_update_slice(
                    own_packed, blocks[side, level][None], (owner, 0, 0)
                )
    other_packed = core_swap(own_packed)
    gathered = jnp.where(
        core == 0,
        jnp.stack([own_packed, other_packed], axis=1),
        jnp.stack([other_packed, own_packed], axis=1),
    ).reshape(2 * CUBE, pack_rows, out_width)
    filters = gathered[:, :filter_rows].reshape(2, 3, 3, in_width, out_width)
    small_full = gathered[:, filter_rows, :small_width].astype(jnp.float32)
    smalls = jnp.concatenate(
        [
            small_full[:, :bias_width].reshape(2, out_width),
            small_full[:, bias_width:].reshape(4, out_width),
        ]
    )
    conv = [
        lax.conv_general_dilated(
            maps[tower],
            filters[tower],
            (1, 1),
            ((1, 1), (1, 1)),
            dimension_numbers=("HWNC", "HWIO", "HWNC"),
            preferred_element_type=jnp.float32,
        )
        for tower in range(2)
    ]
    slope_a, slope_b, pooled, sent = mix(conv, smalls, wide)
    arrived = lax.all_to_all(sent, ("batch", "tower"), split_axis=0, concat_axis=0, tiled=True)
    arrived = arrived.reshape(CUBE, rows, wide)
    dense_all = dense_weight[0].astype(jnp.bfloat16)
    dense_low = [
        jnp.pad(
            dense_all[:, part * half_width : (part + 1) * half_width],
            ((0, wide - dense_rows), (0, 0)),
        )
        for part in range(2)
    ]
    columns = order_rows(place, arrived)
    grad_out = cotangent.astype(jnp.float32) * mask[:, None, None]
    own_stitch = lax.dynamic_index_in_dim(dense_stitch, core, axis=1, keepdims=False)
    other_stitch = lax.dynamic_index_in_dim(dense_stitch, 1 - core, axis=1, keepdims=False)
    own_grad = jnp.sum(own_stitch * grad_out, axis=1).astype(jnp.bfloat16)
    other_grad = core_swap(jnp.sum(other_stitch * grad_out, axis=1).astype(jnp.bfloat16))
    grad_active = [jnp.where(core == part, own_grad, other_grad) for part in range(2)]
    kept, sums = [], [[], []]
    for part in range(2):
        for group in range(2):
            partial = jnp.dot(columns[group], dense_low[part], preferred_element_type=jnp.float32)
            if part:
                partial = held(partial, kept[group])
            partial = partial.astype(jnp.bfloat16).reshape(4, 2, rows, half_width)
            first_sum = reduce_first(partial, group)
            kept.append(first_sum)
            sums[part].append(reduce_second(first_sum, group))
    hidden, grad_full = [], []
    for part in range(2):
        units = slice(part * half_width, (part + 1) * half_width)
        if part:
            sums[1] = [held(group, hidden[0]) for group in sums[1]]
        total = reduce_levels(sums[part]) + dense_bias[:, units]
        if part:
            total = held(total, tops[1])
        hidden.append(total)
        grad_hidden = grad_active[part].astype(jnp.float32) * gate_slope(total)
        tops = gather_levels(grad_hidden.astype(jnp.bfloat16))
        gathered, halves = gather_plane(tops)
        grad_full.append([group.reshape(8 * rows, half_width) for group in gathered])
    active = [smooth_gate(half).astype(jnp.bfloat16) for half in hidden]
    own_active = jnp.where(core == 0, active[0], active[1])
    other_active = core_swap(jnp.where(core == 0, active[1], active[0]))
    own_active = own_active.astype(jnp.float32)[:, None]
    other_active = other_active.astype(jnp.float32)[:, None]
    stitched = own_stitch * own_active + other_stitch * other_active
    stitched = (stitched * mask[:, None, None]).astype(jnp.bfloat16)
    grad_own_stitch = jnp.sum(grad_out * own_active, axis=0)
    grad_other_stitch = jnp.sum(grad_out * other_active, axis=0)
    grad_dense_stitch = jnp.where(
        core == 0,
        jnp.stack([grad_own_stitch, grad_other_stitch], axis=1),
        jnp.stack([grad_other_stitch, grad_own_stitch], axis=1),
    )
    share = lax.all_to_all(
        grad_dense_stitch.reshape(CUBE, -1), "batch", split_axis=0, concat_axis=0, tiled=True
    )
    share = jnp.sum(share, axis=0)
    high = lax.reduce_precision(share, 8, 7)
    share = jnp.concatenate([high, share - high]).reshape(crops, -1)
    share = jnp.pad(share, ((0, 0), (LANES - share.shape[1], 0))).astype(jnp.bfloat16)
    sent = [
        sum(
            lax.dot_general(
                grad_full[part][group],
                dense_low[part],
                (((1,), (1,)), ((), ())),
                preferred_element_type=jnp.float32,
            )
            for part in range(2)
        ).astype(jnp.bfloat16)
        for group in range(2)
    ]
    sent = order_rows(place, *sent, share).reshape(2 * CUBE, crops, wide)
    returned = lax.all_to_all(sent, ("batch", "tower"), split_axis=0, concat_axis=0, tiled=True)
    share = returned.reshape(CUBE, 2, crops, wide)[:, :, :, dense_rows:]
    share = jnp.where(core == 0, share[:, 0], share[:, 1]).astype(jnp.float32).reshape(CUBE, 2, -1)
    grad_dense_stitch = (share[:, 0] + share[:, 1]).reshape(grad_dense_stitch.shape)
    all_columns = jnp.concatenate(columns).T
    states = (dense_weight, dense_weight_first, dense_weight_second)
    update = ()
    for part in range(2):
        update = dense_update(place, all_columns, grad_full[part], *states, part, 2, update)
    small_held = held(smalls, update[4][:, half_width:])
    grad_a, grad_b, grad_small = back(returned, pooled, small_held, (slope_a, slope_b))
    grad_conv = (grad_a, grad_b)
    weight_dims = lax.ConvDimensionNumbers((3, 2, 0, 1), (3, 2, 0, 1), (2, 3, 0, 1))
    grad_filter_weight = [
        lax.conv_general_dilated(
            maps[tower],
            grad_conv[tower],
            (1, 1),
            ((1, 1), (1, 1)),
            dimension_numbers=weight_dims,
            preferred_element_type=jnp.float32,
        )
        .astype(jnp.bfloat16)
        .reshape(CUBE // 2, 2, filter_rows, out_width)
        for tower in range(2)
    ]
    small_grad = jnp.concatenate(
        [grad_small[:2].reshape(2 * CUBE, -1), grad_small[2:].reshape(2 * CUBE, -1)], axis=1
    )
    scales = 1.0 + jnp.arange(8, dtype=jnp.float32)[:, None] / 8.0
    small_grad = jnp.pad(small_grad[:, None] * scales, ((0, 0), (0, 0), (0, out_width - small_width)))
    small_grad = small_grad.astype(jnp.bfloat16).reshape(CUBE, 2, 8, out_width)
    own_filters, other_filters = (
        jnp.concatenate(
            [
                jnp.concatenate(
                    [
                        lax.dynamic_index_in_dim(
                            grad_filter_weight[tower], which, axis=1, keepdims=False
                        )
                        for tower in range(2)
                    ]
                ),
                lax.dynamic_index_in_dim(small_grad, which, axis=1, keepdims=False),
            ],
            axis=1,
        )
        for which in (core, 1 - core)
    )
    blocks = pair_blocks(place, own_filters, core_swap(other_filters))
    firsts = [reduce_first(blocks[group], group) for group in range(2)]
    groups = [reduce_second(firsts[group], group) for group in range(2)]
    block_sums = reduce_levels(groups)
    filter_sums = block_sums[:filter_rows]
    small_sums = jnp.mean(block_sums[filter_rows:] / scales, axis=0)
    input_grad = jnp.stack(
        [
            held(
                lax.conv_general_dilated(
                    grad_conv[tower],
                    filters[tower][::-1, ::-1],
                    (1, 1),
                    ((1, 1), (1, 1)),
                    dimension_numbers=("HWNC", "HWOI", "HWNC"),
                    preferred_element_type=jnp.float32,
                ),
                (blocks[1] if tower == 0 else firsts[1]),
            ).astype(jnp.bfloat16)
            for tower in range(2)
        ]
    )
    input_grad = jnp.transpose(input_grad, (3, 0, 1, 2, 4))
    return (
        stitched,
        input_grad,
        filter_sums,
        small_sums[:bias_width],
        small_sums[bias_width:small_width],
        update[:4],
        update[4][0],
        grad_dense_stitch,
    )


def local(
    crop_maps,
    cotangent,
    crop_counts,
    filter_weight,
    filter_first,
    filter_second,
    conv_filter_bias,
    conv_filter_bias_mean,
    conv_filter_bias_variance,
    pool_stitch,
    pool_stitch_first,
    pool_stitch_second,
    dense_weight,
    dense_weight_first,
    dense_weight_second,
    dense_bias,
    dense_bias_first,
    dense_bias_second,
    dense_stitch,
    dense_stitch_first,
    dense_stitch_second,
):
    gradients = gradients_cube if lax.axis_size("batch") == CUBE else gradients_any
    (
        stitched,
        input_grad,
        filter_sums,
        filter_bias_sums,
        pool_sums,
        dense_update_outs,
        grad_dense_bias,
        grad_dense_stitch,
    ) = gradients(
        crop_maps,
        cotangent,
        crop_counts,
        filter_weight,
        conv_filter_bias,
        pool_stitch,
        dense_weight,
        dense_weight_first,
        dense_weight_second,
        dense_bias,
        dense_stitch,
    )
    updated_conv_weight, updated_conv_weight_mean, updated_conv_weight_variance = (
        decoupled_adam_step(
            filter_weight, filter_first, filter_second, filter_sums, RATE_FILTER, DECAY
        )
    )
    updated_conv_bias, updated_conv_bias_mean, updated_conv_bias_variance = decoupled_adam_step(
        conv_filter_bias,
        conv_filter_bias_mean,
        conv_filter_bias_variance,
        filter_bias_sums,
        BIAS_LEARN_RATE,
        0.0,
    )
    updated_pooling_stitch, updated_pooling_stitch_mean, updated_pooling_stitch_variance = (
        decoupled_adam_step(
            pool_stitch, pool_stitch_first, pool_stitch_second, pool_sums, RATE_STITCH, 0.0
        )
    )
    updated_dense_bias, updated_dense_bias_mean, updated_dense_bias_variance = decoupled_adam_step(
        dense_bias, dense_bias_first, dense_bias_second, grad_dense_bias[None], BIAS_LEARN_RATE, 0.0
    )
    updated_dense_stitch, updated_dense_stitch_mean, updated_dense_stitch_variance = (
        decoupled_adam_step(
            dense_stitch,
            dense_stitch_first,
            dense_stitch_second,
            grad_dense_stitch,
            RATE_STITCH,
            0.0,
        )
    )
    return (
        stitched,
        input_grad,
        updated_conv_weight,
        updated_conv_weight_mean,
        updated_conv_weight_variance,
        updated_conv_weight.astype(jnp.bfloat16),
        updated_conv_bias,
        updated_conv_bias_mean,
        updated_conv_bias_variance,
        updated_pooling_stitch,
        updated_pooling_stitch_mean,
        updated_pooling_stitch_variance,
        *dense_update_outs,
        updated_dense_bias,
        updated_dense_bias_mean,
        updated_dense_bias_variance,
        updated_dense_stitch,
        updated_dense_stitch_mean,
        updated_dense_stitch_variance,
    )


def solution(mesh):
    in_specs = (
        P(("batch", "tower"), None, None, None, None),
        P("batch", None, "tower"),
        P("batch"),
        P(("batch", "tower"), None),
        P(("batch", "tower"), None),
        P(("batch", "tower"), None),
        P(("batch", "tower")),
        P(("batch", "tower")),
        P(("batch", "tower")),
        P(("batch", "tower")),
        P(("batch", "tower")),
        P(("batch", "tower")),
        P("tower", "batch", None),
        P("tower", "batch", None),
        P("tower", "batch", None),
        P("tower", None),
        P("tower", None),
        P("tower", None),
        P(None, None, "tower"),
        P(None, None, "tower"),
        P(None, None, "tower"),
    )
    out_specs = (
        P("batch", None, "tower"),
        P(("batch", "tower"), None, None, None, None),
        P(("batch", "tower"), None),
        P(("batch", "tower"), None),
        P(("batch", "tower"), None),
        P(("batch", "tower"), None),
        P(("batch", "tower")),
        P(("batch", "tower")),
        P(("batch", "tower")),
        P(("batch", "tower")),
        P(("batch", "tower")),
        P(("batch", "tower")),
        P("tower", "batch", None),
        P("tower", "batch", None),
        P("tower", "batch", None),
        P("tower", "batch", None),
        P("tower", None),
        P("tower", None),
        P("tower", None),
        P(None, None, "tower"),
        P(None, None, "tower"),
        P(None, None, "tower"),
    )
    return jax.shard_map(local, mesh=mesh, in_specs=in_specs, out_specs=out_specs, check_vma=False)
```

profile of v0, /device:TPU:0, one launch (start us, length us, event | category | flops | bytes accessed | tf_op | source)
XLA Modules:
  0.0 311.0 jit_solution(8267720338443079185)
XLA Ops:
  2.4 3.1 collective-permute-start
  5.5 2.5 collective-permute-start.4
  9.2 1.6 collective-permute-start.1
  10.7 3.8 %collective-permute-done.4 = bf16[224,256]{1,0:T(8,128)(2,1)S(1)} collective-permute-done((bf16[224,256]{1,0:T(8,128)(2,1)S(1)}, bf16[224,256]{1,0:T(8,128)(2,1)S(1)}, u32[]{:S(2)}, u32[]{:S(2)}) %collective-permute-start.4) | collective-permute-done | bytes 114720 | tf_op jit(solution)/shard_map/ppermute | solution.py:257
  14.5 3.8 %collective-permute-done.3 = bf16[224,256]{1,0:T(8,128)(2,1)S(1)} collective-permute-done((bf16[224,256]{1,0:T(8,128)(2,1)S(1)}, bf16[224,256]{1,0:T(8,128)(2,1)S(1)}, u32[]{:S(2)}, u32[]{:S(2)}) %collective-permute-start.3) | collective-permute-done | bytes 114720 | tf_op jit(solution)/shard_map/ppermute | solution.py:257
  18.3 1.6 collective-permute-start.5
  20.8 6.1 %collective-permute-done.5 = bf16[2,224,256]{2,1,0:T(8,128)(2,1)S(1)} collective-permute-done((bf16[2,224,256]{2,1,0:T(8,128)(2,1)S(1)}, bf16[2,224,256]{2,1,0:T(8,128)(2,1)S(1)}, u32[]{:S(2)}, u32[]{:S(2)}) %collective-permute-start.5) | collective-permute-done | bytes 229408 | tf_op jit(solution)/shard_map/ppermute | solution.py:261
  27.0 1.6 collective-permute-start.6
  28.6 6.5 %collective-permute-done.2 = bf16[2,2,224,256]{3,2,1,0:T(8,128)(2,1)S(1)} collective-permute-done((bf16[2,2,224,256]{3,2,1,0:T(8,128)(2,1)S(1)}, bf16[2,2,224,256]{3,2,1,0:T(8,128)(2,1)S(1)}, u32[]{:S(2)}, u32[]{:S(2)}) %collective-permute-start.2) | collective-permute-done | bytes 458784 | tf_op jit(solution)/shard_map/ppermute | solution.py:261
  36.9 2.3 multiply_reduce_fusion.3
  39.7 2.7 copy.110
  42.4 3.8 %maximum_select_fusion = bf16[16,2,224,256]{3,2,0,1:T(8,128)(2,1)S(1)} fusion(bf16[16,1,224,256]{3,2,0,1:T(8,128)(2,1)} %bitcast.30, bf16[16,1,224,256]{3,2,0,1:T(8,128)(2,1)S(1)} %bitcast.319, pred[]{:T(512)S(6)} %eq.56), kind=kLoop, calls=%fused_computation.5 | loop fusion | flops 5505024 | bytes 7340033 | tf_op jit(solution)/shard_map/jit(_where)/select_n | solution.py:680
  46.8 5.8 %fusion.17.maps_a = f32[13,13,16,256]{3,2,1,0:T(8,128)S(1)} fusion(bf16[3,3,384,256]{3,2,1,0:T(8,128)(2,1)S(1)} %bitcast.330, bf16[2,13,13,16,384]{4,3,2,1,0:T(8,128)(2,1)S(1)} %bitcast.320), kind=kOutput, calls=%fused_computation.31 | convolution fusion | flops 4306501632 | bytes 6615040 | tf_op jit(solution)/shard_map/conv_general_dilated | solution.py:694
  52.6 7.1 %fusion.19.maps_b = f32[13,13,16,256]{3,2,1,0:T(8,128)} fusion(bf16[3,3,384,256]{3,2,1,0:T(8,128)(2,1)S(1)} %bitcast.328, bf16[2,13,13,16,384]{4,3,2,1,0:T(8,128)(2,1)S(1)} %bitcast.321), kind=kOutput, calls=%fused_computation.33 | convolution fusion | flops 4306501632 | bytes 6615040 | tf_op jit(solution)/shard_map/conv_general_dilated | solution.py:694
  60.0 1.8 copy-done.2
  61.8 5.1 %gate_pool_mix.1 = (bf16[13,13,16,256]{3,2,1,0:T(8,128)(2,1)S(1)}, bf16[13,13,16,256]{3,2,1,0:T(8,128)(2,1)S(1)}, bf16[2,36,16,256]{3,2,1,0:T(8,128)(2,1)S(1)}, bf16[32,16,640]{2,1,0:T(8,128)(2,1)}) custom-call(f32[13,13,16,256]{3,2,1,0:T(8,128)S(1)} %fusion.17.maps_a, f32[13,13,16,256]{3,2,1,0:T(8,128)S(1)} %copy-done.2, f32[6,256]{1,0:T(8,128)S(1)} %pad_maximum_fusion.20.small), custom_call_target="tpu_custom_call" | custom-call | flops 41533440 | bytes 8306688 | tf_op jit(solution)/shard_map/gate_pool_mix/pallas_call | solution.py:398
  69.9 4.5 %all-to-all-start = ((bf16[32,16,640]{2,1,0:T(8,128)(2,1)}), bf16[32,16,640]{2,1,0:T(8,128)(2,1)S(1)}, u32[]{:S(2)}, u32[]{:S(2)}) async-start(bf16[32,16,640]{2,1,0:T(8,128)(2,1)} %get-tuple-element.43), calls=%async_computation | async-start | bytes 1310720 | tf_op jit(solution)/shard_map/all_to_all | solution.py:705
  74.5 6.6 %convert_bitcast_fusion = bf16[576,4096]{1,0:T(8,128)(2,1)} fusion(f32[1,576,4096]{2,1,0:T(8,128)} %weight.3), kind=kLoop, calls=%fused_computation | loop fusion | flops 2359296 | bytes 14155776 | tf_op jit(solution)/shard_map/convert_element_type | solution.py:707
  81.1 4.3 %fusion.131 = (bf16[576,2048]{1,0:T(8,128)(2,1)}, bf16[576,2048]{1,0:T(8,128)(2,1)S(1)}) fusion(bf16[576,4096]{1,0:T(8,128)(2,1)} %convert_bitcast_fusion), kind=kLoop, calls=%fused_computation.252 | loop fusion | bytes 9437184 | tf_op jit(solution)/shard_map/slice | solution.py:710
  85.5 6.9 %all-to-all-done = bf16[32,16,640]{2,1,0:T(8,128)(2,1)S(1)} async-done(((bf16[32,16,640]{2,1,0:T(8,128)(2,1)}), bf16[32,16,640]{2,1,0:T(8,128)(2,1)S(1)}, u32[]{:S(2)}, u32[]{:S(2)}) %all-to-all-start) | async-done | bytes 655392 | tf_op jit(solution)/shard_map/all_to_all | solution.py:705
  96.6 1.5 collective-permute-start.8
  98.1 9.9 %collective-permute-done.11 = bf16[2,2,32,2048]{3,2,1,0:T(8,128)(2,1)S(1)} collective-permute-done((bf16[2,2,32,2048]{3,2,1,0:T(8,128)(2,1)S(1)}, bf16[2,2,32,2048]{3,2,1,0:T(8,128)(2,1)S(1)}, u32[]{:S(2)}, u32[]{:S(2)}) %collective-permute-start.11) | collective-permute-done | bytes 524320 | tf_op jit(solution)/shard_map/ppermute | solution.py:261
  108.8 1.8 collective-permute-done.8
  118.8 1.9 collective-permute-start.14
  121.3 2.1 collective-permute-start.10
  124.9 2.1 collective-permute-done.14
  127.0 4.5 %collective-permute-done.13 = bf16[32,2048]{1,0:T(8,128)(2,1)S(1)} collective-permute-done((bf16[32,2048]{1,0:T(8,128)(2,1)S(1)}, bf16[32,2048]{1,0:T(8,128)(2,1)S(1)}, u32[]{:S(2)}, u32[]{:S(2)}) %collective-permute-start.13) | collective-permute-done | bytes 131104 | tf_op jit(solution)/shard_map/ppermute | solution.py:257
  131.9 1.5 collective-permute-start.31
  133.4 2.0 collective-permute-start.30
  142.9 3.8 %collective-permute-done.30 = bf16[32,2048]{1,0:T(8,128)(2,1)S(1)} collective-permute-done((bf16[32,2048]{1,0:T(8,128)(2,1)S(1)}, bf16[32,2048]{1,0:T(8,128)(2,1)S(1)}, u32[]{:S(2)}, u32[]{:S(2)}) %collective-permute-start.30) | collective-permute-done | bytes 131104 | tf_op jit(solution)/shard_map/ppermute | solution.py:257
  148.2 2.0 collective-permute-start.23
  150.3 2.6 collective-permute-start.19
  153.8 1.9 collective-permute-done.32
  156.5 2.3 collective-permute-start.33
  158.8 1.5 collective-permute-done.22
  161.5 1.9 collective-permute-start.35
  163.4 1.6 collective-permute-start.34
  165.4 3.2 %collective-permute-done.27 = bf16[32,2048]{1,0:T(8,128)(2,1)S(1)} collective-permute-done((bf16[32,2048]{1,0:T(8,128)(2,1)S(1)}, bf16[32,2048]{1,0:T(8,128)(2,1)S(1)}, u32[]{:S(2)}, u32[]{:S(2)}) %collective-permute-start.27) | collective-permute-done | bytes 131104 | tf_op jit(solution)/shard_map/ppermute | solution.py:257
  169.9 1.5 collective-permute-start.28
  171.5 1.7 multiply_reduce_fusion.1
  173.9 4.9 %all-to-all-start.1 = ((f32[16,1,512]{2,1,0:T(1,128)}), f32[16,1,512]{2,1,0:T(1,128)S(1)}, u32[]{:S(2)}, u32[]{:S(2)}) async-start(f32[16,1,512]{2,1,0:T(1,128)} %select_n.233), calls=%async_computation.1 | async-start | bytes 65536 | tf_op jit(solution)/shard_map/all_to_all | solution.py:759
  179.9 2.1 collective-permute-start.36
  182.0 4.4 %all-to-all-done.1 = f32[16,1,512]{2,1,0:T(1,128)S(1)} async-done(((f32[16,1,512]{2,1,0:T(1,128)}), f32[16,1,512]{2,1,0:T(1,128)S(1)}, u32[]{:S(2)}, u32[]{:S(2)}) %all-to-all-start.1) | async-done | bytes 32800 | tf_op jit(solution)/shard_map/all_to_all | solution.py:759
  188.7 2.5 collective-permute-start.37
  193.8 5.5 %collective-permute-done.29 = bf16[2,2,32,2048]{3,2,1,0:T(8,128)(2,1)S(1)} collective-permute-done((bf16[2,2,32,2048]{3,2,1,0:T(8,128)(2,1)S(1)}, bf16[2,2,32,2048]{3,2,1,0:T(8,128)(2,1)S(1)}, u32[]{:S(2)}, u32[]{:S(2)}) %collective-permute-start.29) | collective-permute-done | bytes 524320 | tf_op jit(solution)/shard_map/ppermute | solution.py:261
  206.1 5.2 %all-to-all-start.2 = ((bf16[32,16,640]{2,1,0:T(8,128)(2,1)}), bf16[32,16,640]{2,1,0:T(8,128)(2,1)}, u32[]{:S(2)}, u32[]{:S(2)}) async-start(bf16[32,16,640]{2,1,0:T(8,128)(2,1)} %bitcast.316), calls=%async_computation.2 | async-start | bytes 1310720 | tf_op jit(solution)/shard_map/all_to_all | solution.py:779
  211.4 1.9 copy.89
  216.5 11.3 %dense_update.2 = (f32[1,576,4096]{2,1,0:T(8,128)}, f32[1,576,4096]{2,1,0:T(8,128)}, f32[1,576,4096]{2,1,0:T(8,128)}, bf16[1,576,4096]{2,1,0:T(8,128)(2,1)}, f32[1,4096]{1,0:T(1,128)S(1)}) custom-call(s32[3]{0:T(128)S(1)} %pad_add_fusion.place.order, bf16[640,512]{1,0:T(8,128)(2,1)S(1)} %maximum_bitcast_fusion.1.columns, bf16[256,2048]{1,0:T(8,128)(2,1)S(1)} %bitcast.312, ...), custom_call_target="tpu_custom_call" | custom-call | flops 1342177280 | bytes 30670848 | tf_op jit(solution)/shard_map/dense_update/pallas_call | solution.py:611
  227.9 11.4 %dense_update.3 = (f32[1,576,4096]{2,1,0:T(8,128)}, f32[1,576,4096]{2,1,0:T(8,128)}, f32[1,576,4096]{2,1,0:T(8,128)}, bf16[1,576,4096]{2,1,0:T(8,128)(2,1)}, f32[1,4096]{1,0:T(1,128)S(1)}) custom-call(s32[3]{0:T(128)S(1)} %pad_add_fusion.place.order, ...), custom_call_target="tpu_custom_call", output_to_operand_aliasing={{0}: (7, {}), {1}: (8, {}), {2}: (9, {}), {3}: (10, {}), {4... | custom-call | flops 1342177280 | bytes 30670848 | tf_op jit(solution)/shard_map/dense_update/pallas_call | solution.py:611
  243.8 3.2 %pool_gradient.1 = (bf16[13,13,16,256]{3,2,1,0:T(8,128)(2,1)S(1)}, bf16[13,13,16,256]{3,2,1,0:T(8,128)(2,1)S(1)}, f32[6,256]{1,0:T(8,128)S(1)}) custom-call(bf16[32,16,640]{2,1,0:T(8,128)(2,1)} %all-to-all-done.2.returned, bf16[2,36,16,256]{3,2,1,0:T(8,128)(2,1)S(1)} %copy-done.9, f32[6,256]{1,0:T(8,128)S(1)} %broadcast_select_fusion.1.small, ...), custom_call_target="tpu_custom_call" | custom-call | flops 13844480 | bytes 5537792 | tf_op jit(solution)/shard_map/pool_gradient/pallas_call | solution.py:501
  248.5 7.0 %fusion.20 = bf16[3,3,384,256]{3,2,1,0:T(8,128)(2,1)S(1)} fusion(bf16[13,13,16,256]{3,2,1,0:T(8,128)(2,1)S(1)} %get-tuple-element.56, bf16[2,13,13,16,384]{4,3,2,1,0:T(8,128)(2,1)} %bitcast.322), kind=kOutput, calls=%fused_computation.34 | convolution fusion | flops 4307386368 | bytes 5230592 | tf_op jit(solution)/shard_map/conv_general_dilated | solution.py:793
  255.6 5.3 %fusion.21 = bf16[3,3,384,256]{3,2,1,0:T(8,128)(2,1)S(1)} fusion(bf16[13,13,16,256]{3,2,1,0:T(8,128)(2,1)S(1)} %copy-done.12, bf16[2,13,13,16,384]{4,3,2,1,0:T(8,128)(2,1)S(1)} %bitcast.323), kind=kOutput, calls=%fused_computation.35 | convolution fusion | flops 4307386368 | bytes 5230592 | tf_op jit(solution)/shard_map/conv_general_dilated | solution.py:793
  260.9 1.5 dynamic-slice_bitcast_fusion
  266.0 1.9 pad_maximum_fusion.own
  270.1 1.7 collective-permute-start.39
  273.2 1.5 collective-permute-start.40
  274.7 6.8 %fusion.14 = bf16[1,13,13,16,384]{4,3,2,1,0:T(8,128)(2,1)S(1)} fusion(pred[]{:T(512)} %bitcast.100, bf16[13,13,16,256]{3,2,1,0:T(8,128)(2,1)S(1)} %copy-done.13, bf16[3,3,384,256]{3,2,1,0:T(8,128)(2,1)S(1)} %bitcast.331), kind=kOutput, calls=%fused_computation.24 | convolution fusion | flops 4308578304 | bytes 5230593 | tf_op jit(solution)/shard_map/conv_general_dilated | solution.py:837
  284.8 1.8 collective-permute-start.43
  286.6 7.2 %fusion.15 = bf16[1,13,13,16,384]{4,3,2,1,0:T(8,128)(2,1)S(1)} fusion(pred[]{:T(512)} %bitcast.102, bf16[13,13,16,256]{3,2,1,0:T(8,128)(2,1)S(1)} %get-tuple-element.56, bf16[3,3,384,256]{3,2,1,0:T(8,128)(2,1)S(1)} %bitcast.329), kind=kOutput, calls=%fused_computation.25 | convolution fusion | flops 4308578304 | bytes 5230593 | tf_op jit(solution)/shard_map/conv_general_dilated | solution.py:837
  293.9 1.5 collective-permute-start.41
  295.5 3.5 %collective-permute-start.45 = (bf16[224,256]{1,0:T(8,128)(2,1)S(1)}, bf16[224,256]{1,0:T(8,128)(2,1)S(1)}, u32[]{:S(2)}, u32[]{:S(2)}) collective-permute-start(bf16[224,256]{1,0:T(8,128)(2,1)S(1)} %get-tuple-element.206), channel_id=1, source_target_pairs={{0,24},{2,26},{4,28},{6,30},{8,16},{10,18},{12,20},{14,22},{16,8},... | collective-permute-start | bytes 344072 | tf_op jit(solution)/shard_map/ppermute | solution.py:257
  299.0 1.8 collective-permute-done.41
  300.9 1.5 collective-permute-start.42
  302.9 5.2 %copy.96 = bf16[16,2,13,13,384]{4,1,3,2,0:T(2,128)(2,1)} copy(bf16[16,2,13,13,384]{4,0,3,2,1:T(8,128)(2,1)S(1)} %maximum_bitcast_fusion) | data formatting | bytes 8306688
  (301 shorter events, 66.0 us)
Async XLA Ops:
  2.4 6.7 %collective-permute-start = (bf16[224,256]{1,0:T(8,128)(2,1)S(1)}, bf16[224,256]{1,0:T(8,128)(2,1)S(1)}, u32[]{:S(2)}, u32[]{:S(2)}) collective-permute-start(bf16[224,256]{1,0:T(8,128)(2,1)S(1)} %pad_maximum_fusion.18), channel_id=1, source_target_pairs={{0,8},{2,10},{4,12},{6,14},{8,0},{10,2},{12,4},{14,6},{16,24},{18,... | collective-permute-start | bytes 344072 | tf_op jit(solution)/shard_map/ppermute | solution.py:257
  5.5 9.0 %collective-permute-start.4 = (bf16[224,256]{1,0:T(8,128)(2,1)S(1)}, bf16[224,256]{1,0:T(8,128)(2,1)S(1)}, u32[]{:S(2)}, u32[]{:S(2)}) collective-permute-start(bf16[224,256]{1,0:T(8,128)(2,1)S(1)} %pad_maximum_fusion.18), channel_id=1, source_target_pairs={{0,24},{2,26},{4,28},{6,30},{8,16},{10,18},{12,20},{14,22},{16,8},... | collective-permute-start | bytes 344072 | tf_op jit(solution)/shard_map/ppermute | solution.py:257
  8.0 10.3 %collective-permute-start.3 = (bf16[224,256]{1,0:T(8,128)(2,1)S(1)}, bf16[224,256]{1,0:T(8,128)(2,1)S(1)}, u32[]{:S(2)}, u32[]{:S(2)}) collective-permute-start(bf16[224,256]{1,0:T(8,128)(2,1)S(1)} %pad_maximum_fusion.18), channel_id=1, source_target_pairs={{0,16},{2,18},{4,20},{6,22},{8,24},{10,26},{12,28},{14,30},{16,0},... | collective-permute-start | bytes 344072 | tf_op jit(solution)/shard_map/ppermute | solution.py:257
  9.2 11.0 %collective-permute-start.1 = (bf16[2,224,256]{2,1,0:T(8,128)(2,1)S(1)}, bf16[2,224,256]{2,1,0:T(8,128)(2,1)S(1)}, u32[]{:S(2)}, u32[]{:S(2)}) collective-permute-start(bf16[2,224,256]{2,1,0:T(8,128)(2,1)S(1)} %get-tuple-element.209), channel_id=1, source_target_pairs={{0,2},{2,0},{4,6},{6,4},{8,10},{10,8},{12,14},{14,12},{16,18},{18,... | collective-permute-start | bytes 688136 | tf_op jit(solution)/shard_map/ppermute | solution.py:261
  18.3 8.6 %collective-permute-start.5 = (bf16[2,224,256]{2,1,0:T(8,128)(2,1)S(1)}, bf16[2,224,256]{2,1,0:T(8,128)(2,1)S(1)}, u32[]{:S(2)}, u32[]{:S(2)}) collective-permute-start(bf16[2,224,256]{2,1,0:T(8,128)(2,1)S(1)} %get-tuple-element.207), channel_id=1, source_target_pairs={{0,4},{2,6},{4,0},{6,2},{8,12},{10,14},{12,8},{14,10},{16,20},{18,... | collective-permute-start | bytes 688136 | tf_op jit(solution)/shard_map/ppermute | solution.py:261
  20.2 16.3 %copy-start.51 = (s32[16]{0:T(128)S(1)}, s32[16]{0:T(128)}, u32[]{:S(2)}) copy-start(s32[16]{0:T(128)} %param.23) | copy-start | bytes 196
  20.2 14.9 %collective-permute-start.2 = (bf16[2,2,224,256]{3,2,1,0:T(8,128)(2,1)S(1)}, bf16[2,2,224,256]{3,2,1,0:T(8,128)(2,1)S(1)}, u32[]{:S(2)}, u32[]{:S(2)}) collective-permute-start(bf16[2,2,224,256]{3,2,1,0:T(8,128)(2,1)S(1)} %pad_maximum_fusion.10), channel_id=1, source_target_pairs={{0,4},{2,6},{4,0},{6,2},{8,12},{10,14},{12,8},{14,10},{16,20},{18,... | collective-permute-start | bytes 1376264 | tf_op jit(solution)/shard_map/ppermute | solution.py:261
  26.9 9.9 %copy-start.35 = (f32[2,2,2048]{2,1,0:T(2,128)S(1)}, f32[2,2,2048]{2,1,0:T(2,128)}, u32[]{:S(2)}) copy-start(f32[2,2,2048]{2,1,0:T(2,128)} %param.39) | copy-start | bytes 98308
  26.9 10.0 %copy-start.27 = (bf16[32,2,2048]{2,1,0:T(2,128)(2,1)S(1)}, bf16[32,2,2048]{2,1,0:T(2,128)(2,1)}, u32[]{:S(2)}) copy-start(bf16[32,2,2048]{2,1,0:T(2,128)(2,1)} %param.22) | copy-start | bytes 786436
  27.0 9.3 %collective-permute-start.6 = (bf16[2,2,224,256]{3,2,1,0:T(8,128)(2,1)S(1)}, bf16[2,2,224,256]{3,2,1,0:T(8,128)(2,1)S(1)}, u32[]{:S(2)}, u32[]{:S(2)}) collective-permute-start(bf16[2,2,224,256]{3,2,1,0:T(8,128)(2,1)S(1)} %pad_maximum_fusion.11), channel_id=1, source_target_pairs={{0,2},{2,0},{4,6},{6,4},{8,10},{10,8},{12,14},{14,12},{16,18},{18,... | collective-permute-start | bytes 1376264 | tf_op jit(solution)/shard_map/ppermute | solution.py:261
  36.4 6.0 %collective-permute-start.7 = (bf16[16,224,256]{2,1,0:T(8,128)(2,1)S(1)}, bf16[16,224,256]{2,1,0:T(8,128)(2,1)}, u32[]{:S(2)}, u32[]{:S(2)}) collective-permute-start(bf16[16,224,256]{2,1,0:T(8,128)(2,1)S(1)} %fusion.83), channel_id=1, source_target_pairs={{0,1},{1,0},{2,3},{3,2},{4,5},{5,4},{6,7},{7,6},{8,9},{9,8},{10,11... | collective-permute-start | bytes 5505032 | tf_op jit(solution)/shard_map/ppermute | solution.py:63
  39.2 84.4 %collective-permute-start.15 = (bf16[32,2048]{1,0:T(8,128)(2,1)}, bf16[32,2048]{1,0:T(8,128)(2,1)}, u32[]{:S(2)}, u32[]{:S(2)}) collective-permute-start(bf16[32,2048]{1,0:T(8,128)(2,1)} %get-tuple-element.155), channel_id=1, source_target_pairs={{0,1},{1,0},{2,3},{3,2},{4,5},{5,4},{6,7},{7,6},{8,9},{9,8},{10,11... | collective-permute-start | bytes 393224 | tf_op jit(solution)/shard_map/ppermute | solution.py:63
  42.4 10.2 %copy-start.14 = (bf16[16,2,13,13,384]{4,0,3,2,1:T(8,128)(2,1)}, bf16[16,2,13,13,384]{4,0,3,2,1:T(8,128)(2,1)S(1)}, u32[]{:S(2)}) copy-start(bf16[16,2,13,13,384]{4,0,3,2,1:T(8,128)(2,1)S(1)} %copy.110) | copy-start | bytes 12460036
  69.9 22.4 %all-to-all-start = ((bf16[32,16,640]{2,1,0:T(8,128)(2,1)}), bf16[32,16,640]{2,1,0:T(8,128)(2,1)S(1)}, u32[]{:S(2)}, u32[]{:S(2)}) async-start(bf16[32,16,640]{2,1,0:T(8,128)(2,1)} %get-tuple-element.43), calls=%async_computation | async-start | bytes 1310720 | tf_op jit(solution)/shard_map/all_to_all | solution.py:705
  85.5 10.1 %copy-start.16 = (bf16[576,2048]{1,0:T(8,128)(2,1)}, bf16[576,2048]{1,0:T(8,128)(2,1)S(1)}, u32[]{:S(2)}) copy-start(bf16[576,2048]{1,0:T(8,128)(2,1)S(1)} %get-tuple-element.177) | copy-start | bytes 7077892
  93.0 21.1 %copy-start.10 = (bf16[256,640]{1,0:T(8,128)(2,1)}, bf16[256,640]{1,0:T(8,128)(2,1)S(1)}, u32[]{:S(2)}) copy-start(bf16[256,640]{1,0:T(8,128)(2,1)S(1)} %get-tuple-element.45) | copy-start | bytes 983044
  94.1 14.0 %collective-permute-start.11 = (bf16[2,2,32,2048]{3,2,1,0:T(8,128)(2,1)S(1)}, bf16[2,2,32,2048]{3,2,1,0:T(8,128)(2,1)S(1)}, u32[]{:S(2)}, u32[]{:S(2)}) collective-permute-start(bf16[2,2,32,2048]{3,2,1,0:T(8,128)(2,1)S(1)} %bitcast.353), channel_id=1, source_target_pairs={{0,2},{2,0},{4,6},{6,4},{8,10},{10,8},{12,14},{14,12},{16,18},{18,... | collective-permute-start | bytes 1572872 | tf_op jit(solution)/shard_map/ppermute | solution.py:261
  96.6 13.9 %collective-permute-start.8 = (bf16[2,2,32,2048]{3,2,1,0:T(8,128)(2,1)S(1)}, bf16[2,2,32,2048]{3,2,1,0:T(8,128)(2,1)S(1)}, u32[]{:S(2)}, u32[]{:S(2)}) collective-permute-start(bf16[2,2,32,2048]{3,2,1,0:T(8,128)(2,1)S(1)} %bitcast.354), channel_id=1, source_target_pairs={{0,4},{2,6},{4,0},{6,2},{8,12},{10,14},{12,8},{14,10},{16,20},{18,... | collective-permute-start | bytes 1572872 | tf_op jit(solution)/shard_map/ppermute | solution.py:261
  111.2 7.6 %collective-permute-start.12 = (bf16[2,32,2048]{2,1,0:T(8,128)(2,1)S(1)}, bf16[2,32,2048]{2,1,0:T(8,128)(2,1)S(1)}, u32[]{:S(2)}, u32[]{:S(2)}) collective-permute-start(bf16[2,32,2048]{2,1,0:T(8,128)(2,1)S(1)} %fusion.62), channel_id=1, source_target_pairs={{0,4},{2,6},{4,0},{6,2},{8,12},{10,14},{12,8},{14,10},{16,20},{18,... | collective-permute-start | bytes 786440 | tf_op jit(solution)/shard_map/ppermute | solution.py:261
  112.0 9.3 %collective-permute-start.9 = (bf16[2,32,2048]{2,1,0:T(8,128)(2,1)S(1)}, bf16[2,32,2048]{2,1,0:T(8,128)(2,1)S(1)}, u32[]{:S(2)}, u32[]{:S(2)}) collective-permute-start(bf16[2,32,2048]{2,1,0:T(8,128)(2,1)S(1)} %fusion.61), channel_id=1, source_target_pairs={{0,2},{2,0},{4,6},{6,4},{8,10},{10,8},{12,14},{14,12},{16,18},{18,... | collective-permute-start | bytes 786440 | tf_op jit(solution)/shard_map/ppermute | solution.py:261
  115.2 22.0 %collective-permute-start.20 = (bf16[2,2,32,2048]{3,2,1,0:T(8,128)(2,1)S(1)}, bf16[2,2,32,2048]{3,2,1,0:T(8,128)(2,1)S(1)}, u32[]{:S(2)}, u32[]{:S(2)}) collective-permute-start(bf16[2,2,32,2048]{3,2,1,0:T(8,128)(2,1)S(1)} %bitcast.351), channel_id=1, source_target_pairs={{0,2},{2,0},{4,6},{6,4},{8,10},{10,8},{12,14},{14,12},{16,18},{18,... | collective-permute-start | bytes 1572872 | tf_op jit(solution)/shard_map/ppermute | solution.py:261
  118.8 8.2 %collective-permute-start.14 = (bf16[32,2048]{1,0:T(8,128)(2,1)S(1)}, bf16[32,2048]{1,0:T(8,128)(2,1)S(1)}, u32[]{:S(2)}, u32[]{:S(2)}) collective-permute-start(bf16[32,2048]{1,0:T(8,128)(2,1)S(1)} %get-tuple-element.204), channel_id=1, source_target_pairs={{0,24},{2,26},{4,28},{6,30},{8,16},{10,18},{12,20},{14,22},{16,8},... | collective-permute-start | bytes 393224 | tf_op jit(solution)/shard_map/ppermute | solution.py:257
  120.8 10.8 %collective-permute-start.13 = (bf16[32,2048]{1,0:T(8,128)(2,1)S(1)}, bf16[32,2048]{1,0:T(8,128)(2,1)S(1)}, u32[]{:S(2)}, u32[]{:S(2)}) collective-permute-start(bf16[32,2048]{1,0:T(8,128)(2,1)S(1)} %get-tuple-element.203), channel_id=1, source_target_pairs={{0,16},{2,18},{4,20},{6,22},{8,24},{10,26},{12,28},{14,30},{16,0},... | collective-permute-start | bytes 393224 | tf_op jit(solution)/shard_map/ppermute | solution.py:257
  121.3 10.2 %collective-permute-start.10 = (bf16[32,2048]{1,0:T(8,128)(2,1)S(1)}, bf16[32,2048]{1,0:T(8,128)(2,1)S(1)}, u32[]{:S(2)}, u32[]{:S(2)}) collective-permute-start(bf16[32,2048]{1,0:T(8,128)(2,1)S(1)} %fusion.80), channel_id=1, source_target_pairs={{0,8},{2,10},{4,12},{6,14},{8,0},{10,2},{12,4},{14,6},{16,24},{18,... | collective-permute-start | bytes 393224 | tf_op jit(solution)/shard_map/ppermute | solution.py:257
  123.6 15.2 %collective-permute-start.17 = (bf16[2,2,32,2048]{3,2,1,0:T(8,128)(2,1)S(1)}, bf16[2,2,32,2048]{3,2,1,0:T(8,128)(2,1)S(1)}, u32[]{:S(2)}, u32[]{:S(2)}) collective-permute-start(bf16[2,2,32,2048]{3,2,1,0:T(8,128)(2,1)S(1)} %bitcast.352), channel_id=1, source_target_pairs={{0,4},{2,6},{4,0},{6,2},{8,12},{10,14},{12,8},{14,10},{16,20},{18,... | collective-permute-start | bytes 1572872 | tf_op jit(solution)/shard_map/ppermute | solution.py:261
  131.9 7.8 %collective-permute-start.16 = (bf16[32,2048]{1,0:T(8,128)(2,1)S(1)}, bf16[32,2048]{1,0:T(8,128)(2,1)S(1)}, u32[]{:S(2)}, u32[]{:S(2)}) collective-permute-start(bf16[32,2048]{1,0:T(8,128)(2,1)S(1)} %get-tuple-element.174), channel_id=1, source_target_pairs={{0,8},{2,10},{4,12},{6,14},{8,0},{10,2},{12,4},{14,6},{16,24},{18,... | collective-permute-start | bytes 393224 | tf_op jit(solution)/shard_map/ppermute | solution.py:257
  131.9 11.0 %collective-permute-start.31 = (bf16[32,2048]{1,0:T(8,128)(2,1)S(1)}, bf16[32,2048]{1,0:T(8,128)(2,1)S(1)}, u32[]{:S(2)}, u32[]{:S(2)}) collective-permute-start(bf16[32,2048]{1,0:T(8,128)(2,1)S(1)} %get-tuple-element.174), channel_id=1, source_target_pairs={{0,24},{2,26},{4,28},{6,30},{8,16},{10,18},{12,20},{14,22},{16,8},... | collective-permute-start | bytes 393224 | tf_op jit(solution)/shard_map/ppermute | solution.py:257
  133.4 13.3 %collective-permute-start.30 = (bf16[32,2048]{1,0:T(8,128)(2,1)S(1)}, bf16[32,2048]{1,0:T(8,128)(2,1)S(1)}, u32[]{:S(2)}, u32[]{:S(2)}) collective-permute-start(bf16[32,2048]{1,0:T(8,128)(2,1)S(1)} %get-tuple-element.174), channel_id=1, source_target_pairs={{0,16},{2,18},{4,20},{6,22},{8,24},{10,26},{12,28},{14,30},{16,0},... | collective-permute-start | bytes 393224 | tf_op jit(solution)/shard_map/ppermute | solution.py:257
  137.4 10.7 %collective-permute-start.21 = (bf16[2,32,2048]{2,1,0:T(8,128)(2,1)S(1)}, bf16[2,32,2048]{2,1,0:T(8,128)(2,1)S(1)}, u32[]{:S(2)}, u32[]{:S(2)}) collective-permute-start(bf16[2,32,2048]{2,1,0:T(8,128)(2,1)S(1)} %fusion.64), channel_id=1, source_target_pairs={{0,4},{2,6},{4,0},{6,2},{8,12},{10,14},{12,8},{14,10},{16,20},{18,... | collective-permute-start | bytes 786440 | tf_op jit(solution)/shard_map/ppermute | solution.py:261
  138.9 11.3 %collective-permute-start.18 = (bf16[2,32,2048]{2,1,0:T(8,128)(2,1)S(1)}, bf16[2,32,2048]{2,1,0:T(8,128)(2,1)S(1)}, u32[]{:S(2)}, u32[]{:S(2)}) collective-permute-start(bf16[2,32,2048]{2,1,0:T(8,128)(2,1)S(1)} %fusion.63), channel_id=1, source_target_pairs={{0,2},{2,0},{4,6},{6,4},{8,10},{10,8},{12,14},{14,12},{16,18},{18,... | collective-permute-start | bytes 786440 | tf_op jit(solution)/shard_map/ppermute | solution.py:261
  141.5 11.3 %collective-permute-start.25 = (bf16[2,32,2048]{2,1,0:T(8,128)(2,1)S(1)}, bf16[2,32,2048]{2,1,0:T(8,128)(2,1)S(1)}, u32[]{:S(2)}, u32[]{:S(2)}) collective-permute-start(bf16[2,32,2048]{2,1,0:T(8,128)(2,1)S(1)} %get-tuple-element.198), channel_id=1, source_target_pairs={{0,2},{2,0},{4,6},{6,4},{8,10},{10,8},{12,14},{14,12},{16,18},{18,... | collective-permute-start | bytes 786440 | tf_op jit(solution)/shard_map/ppermute | solution.py:261
  146.8 8.8 %collective-permute-start.32 = (bf16[2,32,2048]{2,1,0:T(8,128)(2,1)S(1)}, bf16[2,32,2048]{2,1,0:T(8,128)(2,1)S(1)}, u32[]{:S(2)}, u32[]{:S(2)}) collective-permute-start(bf16[2,32,2048]{2,1,0:T(8,128)(2,1)S(1)} %get-tuple-element.194), channel_id=1, source_target_pairs={{0,4},{2,6},{4,0},{6,2},{8,12},{10,14},{12,8},{14,10},{16,20},{18,... | collective-permute-start | bytes 786440 | tf_op jit(solution)/shard_map/ppermute | solution.py:261
  148.2 10.6 %collective-permute-start.23 = (bf16[32,2048]{1,0:T(8,128)(2,1)S(1)}, bf16[32,2048]{1,0:T(8,128)(2,1)S(1)}, u32[]{:S(2)}, u32[]{:S(2)}) collective-permute-start(bf16[32,2048]{1,0:T(8,128)(2,1)S(1)} %get-tuple-element.202), channel_id=1, source_target_pairs={{0,24},{2,26},{4,28},{6,30},{8,16},{10,18},{12,20},{14,22},{16,8},... | collective-permute-start | bytes 393224 | tf_op jit(solution)/shard_map/ppermute | solution.py:257
  150.2 10.1 %collective-permute-start.22 = (bf16[32,2048]{1,0:T(8,128)(2,1)S(1)}, bf16[32,2048]{1,0:T(8,128)(2,1)S(1)}, u32[]{:S(2)}, u32[]{:S(2)}) collective-permute-start(bf16[32,2048]{1,0:T(8,128)(2,1)S(1)} %get-tuple-element.201), channel_id=1, source_target_pairs={{0,16},{2,18},{4,20},{6,22},{8,24},{10,26},{12,28},{14,30},{16,0},... | collective-permute-start | bytes 393224 | tf_op jit(solution)/shard_map/ppermute | solution.py:257
  150.3 10.0 %collective-permute-start.19 = (bf16[32,2048]{1,0:T(8,128)(2,1)S(1)}, bf16[32,2048]{1,0:T(8,128)(2,1)S(1)}, u32[]{:S(2)}, u32[]{:S(2)}) collective-permute-start(bf16[32,2048]{1,0:T(8,128)(2,1)S(1)} %fusion.81), channel_id=1, source_target_pairs={{0,8},{2,10},{4,12},{6,14},{8,0},{10,2},{12,4},{14,6},{16,24},{18,... | collective-permute-start | bytes 393224 | tf_op jit(solution)/shard_map/ppermute | solution.py:257
  152.9 38.4 %collective-permute-start.26 = (bf16[2,2,32,2048]{3,2,1,0:T(8,128)(2,1)S(1)}, bf16[2,2,32,2048]{3,2,1,0:T(8,128)(2,1)}, u32[]{:S(2)}, u32[]{:S(2)}) collective-permute-start(bf16[2,2,32,2048]{3,2,1,0:T(8,128)(2,1)S(1)} %pad_maximum_fusion.6), channel_id=1, source_target_pairs={{0,4},{2,6},{4,0},{6,2},{8,12},{10,14},{12,8},{14,10},{16,20},{18,... | collective-permute-start | bytes 1572872 | tf_op jit(solution)/shard_map/ppermute | solution.py:261
  155.6 13.0 %copy-start.29 = (bf16[2,32,2048]{2,1,0:T(8,128)(2,1)}, bf16[2,32,2048]{2,1,0:T(8,128)(2,1)S(1)}, u32[]{:S(2)}) copy-start(bf16[2,32,2048]{2,1,0:T(8,128)(2,1)S(1)} %collective-permute-done.32) | copy-start | bytes 786436
  156.5 15.0 %copy-start.28 = (bf16[32,2,2048]{2,1,0:T(2,128)(2,1)S(1)}, bf16[32,2,2048]{2,1,0:T(2,128)(2,1)}, u32[]{:S(2)}) copy-start(bf16[32,2,2048]{2,1,0:T(2,128)(2,1)} %param.22) | copy-start | bytes 786436
  156.5 36.0 %collective-permute-start.33 = (bf16[2,2,32,2048]{3,2,1,0:T(8,128)(2,1)}, bf16[2,2,32,2048]{3,2,1,0:T(8,128)(2,1)}, u32[]{:S(2)}, u32[]{:S(2)}) collective-permute-start(bf16[2,2,32,2048]{3,2,1,0:T(8,128)(2,1)} %pad_maximum_fusion.8), channel_id=1, source_target_pairs={{0,2},{2,0},{4,6},{6,4},{8,10},{10,8},{12,14},{14,12},{16,18},{18,... | collective-permute-start | bytes 1572872 | tf_op jit(solution)/shard_map/ppermute | solution.py:261
  161.4 7.1 %collective-permute-start.27 = (bf16[32,2048]{1,0:T(8,128)(2,1)S(1)}, bf16[32,2048]{1,0:T(8,128)(2,1)S(1)}, u32[]{:S(2)}, u32[]{:S(2)}) collective-permute-start(bf16[32,2048]{1,0:T(8,128)(2,1)S(1)} %fusion.60), channel_id=1, source_target_pairs={{0,8},{2,10},{4,12},{6,14},{8,0},{10,2},{12,4},{14,6},{16,24},{18,... | collective-permute-start | bytes 393224 | tf_op jit(solution)/shard_map/ppermute | solution.py:257
  161.5 17.4 %collective-permute-start.35 = (bf16[32,2048]{1,0:T(8,128)(2,1)S(1)}, bf16[32,2048]{1,0:T(8,128)(2,1)}, u32[]{:S(2)}, u32[]{:S(2)}) collective-permute-start(bf16[32,2048]{1,0:T(8,128)(2,1)S(1)} %fusion.60), channel_id=1, source_target_pairs={{0,24},{2,26},{4,28},{6,30},{8,16},{10,18},{12,20},{14,22},{16,8},... | collective-permute-start | bytes 393224 | tf_op jit(solution)/shard_map/ppermute | solution.py:257
  163.4 15.5 %collective-permute-start.34 = (bf16[32,2048]{1,0:T(8,128)(2,1)S(1)}, bf16[32,2048]{1,0:T(8,128)(2,1)}, u32[]{:S(2)}, u32[]{:S(2)}) collective-permute-start(bf16[32,2048]{1,0:T(8,128)(2,1)S(1)} %fusion.60), channel_id=1, source_target_pairs={{0,16},{2,18},{4,20},{6,22},{8,24},{10,26},{12,28},{14,30},{16,0},... | collective-permute-start | bytes 393224 | tf_op jit(solution)/shard_map/ppermute | solution.py:257
  168.6 1.3 collective-permute-start.24
  169.9 16.7 %collective-permute-start.28 = (bf16[2,32,2048]{2,1,0:T(8,128)(2,1)S(1)}, bf16[2,32,2048]{2,1,0:T(8,128)(2,1)S(1)}, u32[]{:S(2)}, u32[]{:S(2)}) collective-permute-start(bf16[2,32,2048]{2,1,0:T(8,128)(2,1)S(1)} %get-tuple-element.200), channel_id=1, source_target_pairs={{0,2},{2,0},{4,6},{6,4},{8,10},{10,8},{12,14},{14,12},{16,18},{18,... | collective-permute-start | bytes 786440 | tf_op jit(solution)/shard_map/ppermute | solution.py:261
  173.9 12.4 %all-to-all-start.1 = ((f32[16,1,512]{2,1,0:T(1,128)}), f32[16,1,512]{2,1,0:T(1,128)S(1)}, u32[]{:S(2)}, u32[]{:S(2)}) async-start(f32[16,1,512]{2,1,0:T(1,128)} %select_n.233), calls=%async_computation.1 | async-start | bytes 65536 | tf_op jit(solution)/shard_map/all_to_all | solution.py:759
  179.9 12.5 %copy-start.20 = (bf16[1,2,32,2048]{3,2,1,0:T(8,128)(2,1)}, bf16[1,2,32,2048]{3,2,1,0:T(8,128)(2,1)S(1)}, u32[]{:S(2)}) copy-start(bf16[1,2,32,2048]{3,2,1,0:T(8,128)(2,1)S(1)} %get-tuple-element.195) | copy-start | bytes 786436
  179.9 8.8 %collective-permute-start.36 = (bf16[2,32,2048]{2,1,0:T(8,128)(2,1)S(1)}, bf16[2,32,2048]{2,1,0:T(8,128)(2,1)S(1)}, u32[]{:S(2)}, u32[]{:S(2)}) collective-permute-start(bf16[2,32,2048]{2,1,0:T(8,128)(2,1)S(1)} %get-tuple-element.196), channel_id=1, source_target_pairs={{0,4},{2,6},{4,0},{6,2},{8,12},{10,14},{12,8},{14,10},{16,20},{18,... | collective-permute-start | bytes 786440 | tf_op jit(solution)/shard_map/ppermute | solution.py:261
  186.6 12.7 %collective-permute-start.29 = (bf16[2,2,32,2048]{3,2,1,0:T(8,128)(2,1)S(1)}, bf16[2,2,32,2048]{3,2,1,0:T(8,128)(2,1)S(1)}, u32[]{:S(2)}, u32[]{:S(2)}) collective-permute-start(bf16[2,2,32,2048]{3,2,1,0:T(8,128)(2,1)S(1)} %pad_maximum_fusion.7), channel_id=1, source_target_pairs={{0,4},{2,6},{4,0},{6,2},{8,12},{10,14},{12,8},{14,10},{16,20},{18,... | collective-permute-start | bytes 1572872 | tf_op jit(solution)/shard_map/ppermute | solution.py:261
  188.7 12.1 %collective-permute-start.37 = (bf16[2,2,32,2048]{3,2,1,0:T(8,128)(2,1)S(1)}, bf16[2,2,32,2048]{3,2,1,0:T(8,128)(2,1)S(1)}, u32[]{:S(2)}, u32[]{:S(2)}) collective-permute-start(bf16[2,2,32,2048]{3,2,1,0:T(8,128)(2,1)S(1)} %pad_maximum_fusion.9), channel_id=1, source_target_pairs={{0,2},{2,0},{4,6},{6,4},{8,10},{10,8},{12,14},{14,12},{16,18},{18,... | collective-permute-start | bytes 1572872 | tf_op jit(solution)/shard_map/ppermute | solution.py:261
  192.5 7.0 %copy-start.19 = (bf16[576,2048]{1,0:T(8,128)(2,1)S(1)}, bf16[576,2048]{1,0:T(8,128)(2,1)}, u32[]{:S(2)}) copy-start(bf16[576,2048]{1,0:T(8,128)(2,1)} %get-tuple-element.176) | copy-start | bytes 7077892
  193.8 9.8 %copy-start = (bf16[4,2,32,2048]{3,2,1,0:T(8,128)(2,1)}, bf16[4,2,32,2048]{3,2,1,0:T(8,128)(2,1)S(1)}, u32[]{:S(2)}) copy-start(bf16[4,2,32,2048]{3,2,1,0:T(8,128)(2,1)S(1)} %pad_maximum_fusion.4) | copy-start | bytes 3145732
  206.1 34.9 %all-to-all-start.2 = ((bf16[32,16,640]{2,1,0:T(8,128)(2,1)}), bf16[32,16,640]{2,1,0:T(8,128)(2,1)}, u32[]{:S(2)}, u32[]{:S(2)}) async-start(bf16[32,16,640]{2,1,0:T(8,128)(2,1)} %bitcast.316), calls=%async_computation.2 | async-start | bytes 1310720 | tf_op jit(solution)/shard_map/all_to_all | solution.py:779
  211.4 37.0 %copy-start.43 = (f32[8]{0:T(128)}, f32[8]{0:T(128)S(1)}, u32[]{:S(2)}) copy-start(f32[8]{0:T(128)S(1)} %multiply_add_fusion.5) | copy-start | bytes 100
  227.8 13.2 %copy-start.9 = (bf16[2,36,16,256]{3,2,1,0:T(8,128)(2,1)S(1)}, bf16[2,36,16,256]{3,2,1,0:T(8,128)(2,1)}, u32[]{:S(2)}) copy-start(bf16[2,36,16,256]{3,2,1,0:T(8,128)(2,1)} %copy-done.8) | copy-start | bytes 1769476
  248.5 7.1 %copy-start.12 = (bf16[13,13,16,256]{3,2,1,0:T(8,128)(2,1)S(1)}, bf16[13,13,16,256]{3,2,1,0:T(8,128)(2,1)}, u32[]{:S(2)}) copy-start(bf16[13,13,16,256]{3,2,1,0:T(8,128)(2,1)} %copy-done.11) | copy-start | bytes 4153348
  248.5 7.1 %copy-start.15 = (bf16[16,2,13,13,384]{4,0,3,2,1:T(8,128)(2,1)S(1)}, bf16[16,2,13,13,384]{4,0,3,2,1:T(8,128)(2,1)}, u32[]{:S(2)}) copy-start(bf16[16,2,13,13,384]{4,0,3,2,1:T(8,128)(2,1)} %copy-done.14) | copy-start | bytes 12460036
  263.8 4.8 %collective-permute-start.38 = (bf16[16,224,256]{2,1,0:T(8,128)(2,1)}, bf16[16,224,256]{2,1,0:T(8,128)(2,1)S(1)}, u32[]{:S(2)}, u32[]{:S(2)}) collective-permute-start(bf16[16,224,256]{2,1,0:T(8,128)(2,1)} %pad_maximum_fusion.1), channel_id=1, source_target_pairs={{0,1},{1,0},{2,3},{3,2},{4,5},{5,4},{6,7},{7,6},{8,9},{9,8},{10,11... | collective-permute-start | bytes 5505032 | tf_op jit(solution)/shard_map/ppermute | solution.py:63
  270.1 12.8 %collective-permute-start.39 = (bf16[2,2,224,256]{3,2,1,0:T(8,128)(2,1)S(1)}, bf16[2,2,224,256]{3,2,1,0:T(8,128)(2,1)S(1)}, u32[]{:S(2)}, u32[]{:S(2)}) collective-permute-start(bf16[2,2,224,256]{3,2,1,0:T(8,128)(2,1)S(1)} %slice.350), channel_id=1, source_target_pairs={{0,2},{2,0},{4,6},{6,4},{8,10},{10,8},{12,14},{14,12},{16,18},{18,... | collective-permute-start | bytes 1376264 | tf_op jit(solution)/shard_map/ppermute | solution.py:261
  273.2 20.6 %collective-permute-start.40 = (bf16[2,2,224,256]{3,2,1,0:T(8,128)(2,1)S(1)}, bf16[2,2,224,256]{3,2,1,0:T(8,128)(2,1)S(1)}, u32[]{:S(2)}, u32[]{:S(2)}) collective-permute-start(bf16[2,2,224,256]{3,2,1,0:T(8,128)(2,1)S(1)} %slice.353), channel_id=1, source_target_pairs={{0,4},{2,6},{4,0},{6,2},{8,12},{10,14},{12,8},{14,10},{16,20},{18,... | collective-permute-start | bytes 1376264 | tf_op jit(solution)/shard_map/ppermute | solution.py:261
  284.8 10.6 %collective-permute-start.43 = (bf16[2,224,256]{2,1,0:T(8,128)(2,1)S(1)}, bf16[2,224,256]{2,1,0:T(8,128)(2,1)S(1)}, u32[]{:S(2)}, u32[]{:S(2)}) collective-permute-start(bf16[2,224,256]{2,1,0:T(8,128)(2,1)S(1)} %fusion.75), channel_id=1, source_target_pairs={{0,4},{2,6},{4,0},{6,2},{8,12},{10,14},{12,8},{14,10},{16,20},{18,... | collective-permute-start | bytes 688136 | tf_op jit(solution)/shard_map/ppermute | solution.py:261
  293.9 6.9 %collective-permute-start.41 = (bf16[2,224,256]{2,1,0:T(8,128)(2,1)S(1)}, bf16[2,224,256]{2,1,0:T(8,128)(2,1)S(1)}, u32[]{:S(2)}, u32[]{:S(2)}) collective-permute-start(bf16[2,224,256]{2,1,0:T(8,128)(2,1)S(1)} %fusion.74), channel_id=1, source_target_pairs={{0,2},{2,0},{4,6},{6,4},{8,10},{10,8},{12,14},{14,12},{16,18},{18,... | collective-permute-start | bytes 688136 | tf_op jit(solution)/shard_map/ppermute | solution.py:261
  295.5 12.6 %collective-permute-start.45 = (bf16[224,256]{1,0:T(8,128)(2,1)S(1)}, bf16[224,256]{1,0:T(8,128)(2,1)S(1)}, u32[]{:S(2)}, u32[]{:S(2)}) collective-permute-start(bf16[224,256]{1,0:T(8,128)(2,1)S(1)} %get-tuple-element.206), channel_id=1, source_target_pairs={{0,24},{2,26},{4,28},{6,30},{8,16},{10,18},{12,20},{14,22},{16,8},... | collective-permute-start | bytes 344072 | tf_op jit(solution)/shard_map/ppermute | solution.py:257
  299.0 9.1 %collective-permute-start.44 = (bf16[224,256]{1,0:T(8,128)(2,1)S(1)}, bf16[224,256]{1,0:T(8,128)(2,1)S(1)}, u32[]{:S(2)}, u32[]{:S(2)}) collective-permute-start(bf16[224,256]{1,0:T(8,128)(2,1)S(1)} %get-tuple-element.205), channel_id=1, source_target_pairs={{0,16},{2,18},{4,20},{6,22},{8,24},{10,26},{12,28},{14,30},{16,0},... | collective-permute-start | bytes 344072 | tf_op jit(solution)/shard_map/ppermute | solution.py:257
  300.9 7.3 %collective-permute-start.42 = (bf16[224,256]{1,0:T(8,128)(2,1)S(1)}, bf16[224,256]{1,0:T(8,128)(2,1)S(1)}, u32[]{:S(2)}, u32[]{:S(2)}) collective-permute-start(bf16[224,256]{1,0:T(8,128)(2,1)S(1)} %fusion.82), channel_id=1, source_target_pairs={{0,8},{2,10},{4,12},{6,14},{8,0},{10,2},{12,4},{14,6},{16,24},{18,... | collective-permute-start | bytes 344072 | tf_op jit(solution)/shard_map/ppermute | solution.py:257
  (37 other events, 109.5 us)
where the time goes:
time: 315 us; the launch traced here: 311 us
  starting transfers between devices  75.7 us (24%)
  waiting for transfers between devices  73.2 us (23%)
  matrix products  47.3 us (15%)
  other arithmetic  35 us (11%)
  local copies, waits for them, and re-layouts  34.9 us (11%)
  Pallas kernels  33.1 us (11%)
  between operations  11.7 us (4%)
    ppermute x24, waiting for transfers between devices, plane_hop(): return lax.ppermute(values, 'batch', [(i, i ^ offset) for i in range(CUBE)])  37.6 us
    ppermute x24, starting transfers between devices, plane_hop(): return lax.ppermute(values, 'batch', [(i, i ^ offset) for i in range(CUBE)])  33.5 us
    ppermute x18, starting transfers between devices, hop(): lax.ppermute(values, 'batch', [(i, i ^ 4 * level) for i in range(CUBE)])  26.8 us
    ppermute x18, waiting for transfers between devices, hop(): lax.ppermute(values, 'batch', [(i, i ^ 4 * level) for i in range(CUBE)])  23 us
    pallas_call x2, Pallas kernels, dense_update(): pl.pallas_call(dense_kernel, grid=(steps,), out_shape=outs, in_specs=[pl....  22.7 us
    unnamed x108, local copies, waits for them, and re-layouts  19.5 us
    conv_general_dilated x2, matrix products, gradients_cube(): lax.conv_general_dilated(grad_conv[tower], filters[tower][::-1, ::-1], (1...  14 us
    conv_general_dilated x2, matrix products, gradients_cube(): lax.conv_general_dilated(maps[tower], filters[tower], (1, 1), ((1, 1), (1...  12.9 us
  transfers between devices with their start and end apart: 49, of which 22 were waited for; matrix products, arithmetic and copies ran while one was open for 26% of the time, Pallas kernels for 9%

commit v1 on v0

--- a/solution.py
+++ b/solution.py
@@ -335,7 +335,7 @@
             bias = small[tower][None]
             running = [None] * count
             for x in range(width):
-                value = maps[y, x] + bias
+                value = maps[y, x].astype(jnp.float32) + bias
                 square = value * value
                 bend = jnp.tanh(GELU_SCALE * value * (1.0 + GELU_CUBIC * square))
                 half = 0.5 + 0.5 * bend
@@ -580,11 +580,16 @@
     )(place, own, other)
 
 
-def dense_kernel(order, columns, grads_a, grads_b, weight, first, second, *outs):
-    new_weight, new_first, new_second, copy, grad_bias = outs[-5:]
-    rows = grads_a.shape[0]
-    grad = jnp.dot(columns[:, :rows], grads_a[...], preferred_element_type=jnp.float32)
-    grad += jnp.dot(columns[:, rows:], grads_b[...], preferred_element_type=jnp.float32)
+def dense_kernel(columns_a, columns_b, *refs):
+    weight, first, second, new_weight, new_first, new_second, copy, grad_bias = refs[4:]
+    early = pl.program_id(0) < pl.num_programs(0) // 2
+    grads = [jnp.where(early, refs[group][...], refs[2 + group][...]) for group in range(2)]
+    grad = sum(
+        lax.dot_general(
+            columns[...], part, (((0,), (0,)), ((), ())), preferred_element_type=jnp.float32
+        )
+        for columns, part in zip((columns_a, columns_b), grads)
+    )
     updated, mean, square = decoupled_adam_step(
         weight[0], first[0], second[0], grad[: weight.shape[1]], RATE_DENSE, DECAY
     )
@@ -593,16 +598,19 @@
     new_second[0] = square
     copy[0] = updated.astype(jnp.bfloat16)
     grad_bias[...] = jnp.sum(
-        grads_a[...].astype(jnp.float32) + grads_b[...].astype(jnp.float32), axis=0, keepdims=True
-    )
-
-
-def dense_update(order, columns, grads, weight, first, second, part, parts, old):
+        grads[0].astype(jnp.float32) + grads[1].astype(jnp.float32), axis=0, keepdims=True
+    )
+
+
+def dense_update(columns, grads, weight, first, second):
     tile = 1024
     _, rows, units = weight.shape
-    steps = units // tile // parts
-    state = pl.BlockSpec((1, rows, tile), lambda step: (0, 0, part * steps + step))
-    grad = pl.BlockSpec((grads[0].shape[0], tile), lambda step: (0, step))
+    steps = units // tile
+    half = steps // 2
+    state = pl.BlockSpec((1, rows, tile), lambda step: (0, 0, step))
+    block = (grads[0][0].shape[0], tile)
+    early = pl.BlockSpec(block, lambda step: (0, jnp.minimum(step, half - 1)))
+    late = pl.BlockSpec(block, lambda step: (0, jnp.maximum(step - half, 0)))
     outs = [jax.ShapeDtypeStruct(weight.shape, jnp.float32)] * 3
     outs += [
         jax.ShapeDtypeStruct(weight.shape, jnp.bfloat16),
@@ -613,25 +621,24 @@
         grid=(steps,),
         out_shape=outs,
         in_specs=[
-            pl.BlockSpec(memory_space=pltpu.SMEM),
-            pl.BlockSpec(columns.shape, lambda step: (0, 0)),
-            grad,
-            grad,
+            *[pl.BlockSpec(columns[0].shape, lambda step: (0, 0))] * 2,
+            early,
+            early,
+            late,
+            late,
             state,
             state,
             state,
-            *[pl.BlockSpec(memory_space=pl.ANY)] * len(old),
         ],
-        out_specs=[state] * 4 + [pl.BlockSpec((1, tile), lambda step: (0, part * steps + step))],
-        input_output_aliases={7 + i: i for i in range(len(old))},
+        out_specs=[state] * 4 + [pl.BlockSpec((1, tile), lambda step: (0, step))],
         compiler_params=pltpu.CompilerParams(vmem_limit_bytes=48 << 20),
         cost_estimate=pl.CostEstimate(
-            flops=2 * columns.size * units // parts,
-            bytes_accessed=26 * weight.size // parts,
-            transcendentals=weight.size // parts,
+            flops=4 * columns[0].size * units,
+            bytes_accessed=26 * weight.size,
+            transcendentals=weight.size,
         ),
         name="dense_update",
-    )(order, columns, *grads, weight, first, second, *old)
+    )(*columns, *grads[0], *grads[1], weight, first, second)
 
 
 def gradients_cube(
@@ -698,7 +705,7 @@
             ((1, 1), (1, 1)),
             dimension_numbers=("HWNC", "HWIO", "HWNC"),
             preferred_element_type=jnp.float32,
-        )
+        ).astype(jnp.bfloat16)
         for tower in range(2)
     ]
     slope_a, slope_b, pooled, sent = mix(conv, smalls, wide)
@@ -780,12 +787,10 @@
     share = returned.reshape(CUBE, 2, crops, wide)[:, :, :, dense_rows:]
     share = jnp.where(core == 0, share[:, 0], share[:, 1]).astype(jnp.float32).reshape(CUBE, 2, -1)
     grad_dense_stitch = (share[:, 0] + share[:, 1]).reshape(grad_dense_stitch.shape)
-    all_columns = jnp.concatenate(columns).T
-    states = (dense_weight, dense_weight_first, dense_weight_second)
-    update = ()
-    for part in range(2):
-        update = dense_update(place, all_columns, grad_full[part], *states, part, 2, update)
-    small_held = held(smalls, update[4][:, half_width:])
+    update = dense_update(
+        columns, grad_full, dense_weight, dense_weight_first, dense_weight_second
+    )
+    small_held = held(smalls, update[4])
     grad_a, grad_b, grad_small = back(returned, pooled, small_held, (slope_a, slope_b))
     grad_conv = (grad_a, grad_b)
     weight_dims = lax.ConvDimensionNumbers((3, 2, 0, 1), (3, 2, 0, 1), (2, 3, 0, 1))

time: 315 us -> 309 us (0.981)
  local copies, waits for them, and re-layouts: 34.9 us -> 31.6 us
    pallas_call x2 -> x1, Pallas kernels: 22.7 us -> 22.1 us  [dense_update(): pl.pallas_call(dense_kernel, grid=(steps,), out_shape=outs, in_specs=[*[p...]
    unnamed x108 -> x118, local copies, waits for them, and re-layouts: 19.5 us -> 19 us
where the time goes in v1:
time: 309 us; the launch traced here: 305 us
  starting transfers between devices  75.8 us (25%)
  waiting for transfers between devices  72.1 us (23%)
  matrix products  45.4 us (15%)
  other arithmetic  35.4 us (11%)
  Pallas kernels  32.6 us (11%)
  local copies, waits for them, and re-layouts  31.6 us (10%)
  between operations  11.5 us (4%)
    ppermute x24, waiting for transfers between devices, plane_hop(): return lax.ppermute(values, 'batch', [(i, i ^ offset) for i in range(CUBE)])  37.4 us
    ppermute x24, starting transfers between devices, plane_hop(): return lax.ppermute(values, 'batch', [(i, i ^ offset) for i in range(CUBE)])  33.8 us
    ppermute x18, starting transfers between devices, hop(): lax.ppermute(values, 'batch', [(i, i ^ 4 * level) for i in range(CUBE)])  26.7 us
    ppermute x18, waiting for transfers between devices, hop(): lax.ppermute(values, 'batch', [(i, i ^ 4 * level) for i in range(CUBE)])  23 us
    pallas_call x1, Pallas kernels, dense_update(): pl.pallas_call(dense_kernel, grid=(steps,), out_shape=outs, in_specs=[*[p...  22.1 us
    unnamed x118, local copies, waits for them, and re-layouts  19 us
    conv_general_dilated x2, matrix products, gradients_cube(): lax.conv_general_dilated(grad_conv[tower], filters[tower][::-1, ::-1], (1...  14 us
    conv_general_dilated x2, matrix products, gradients_cube(): lax.conv_general_dilated(maps[tower], grad_conv[tower], (1, 1), ((1, 1),...  12.5 us
  transfers between devices with their start and end apart: 49, of which 22 were waited for; matrix products, arithmetic and copies ran while one was open for 26% of the time, Pallas kernels for 9%

profile of v1, /device:TPU:0, one launch (start us, length us, event | category | flops | bytes accessed | tf_op | source)
XLA Modules:
  0.0 304.6 jit_solution(5129361640771343028)
XLA Ops:
  2.4 3.1 %collective-permute-start = (bf16[224,256]{1,0:T(8,128)(2,1)S(1)}, bf16[224,256]{1,0:T(8,128)(2,1)S(1)}, u32[]{:S(2)}, u32[]{:S(2)}) collective-permute-start(bf16[224,256]{1,0:T(8,128)(2,1)S(1)} %pad_maximum_fusion.18), channel_id=1, source_target_pairs={{0,8},{2,10},{4,12},{6,14},{8,0},{10,2},{12,4},{14,6},{16,24},{18,... | collective-permute-start | bytes 344072 | tf_op jit(solution)/shard_map/ppermute | solution.py:257
  5.5 2.5 collective-permute-start.4
  9.2 1.6 collective-permute-start.1
  10.7 3.8 %collective-permute-done.4 = bf16[224,256]{1,0:T(8,128)(2,1)S(1)} collective-permute-done((bf16[224,256]{1,0:T(8,128)(2,1)S(1)}, bf16[224,256]{1,0:T(8,128)(2,1)S(1)}, u32[]{:S(2)}, u32[]{:S(2)}) %collective-permute-start.4) | collective-permute-done | bytes 114720 | tf_op jit(solution)/shard_map/ppermute | solution.py:257
  14.5 3.8 %collective-permute-done.3 = bf16[224,256]{1,0:T(8,128)(2,1)S(1)} collective-permute-done((bf16[224,256]{1,0:T(8,128)(2,1)S(1)}, bf16[224,256]{1,0:T(8,128)(2,1)S(1)}, u32[]{:S(2)}, u32[]{:S(2)}) %collective-permute-start.3) | collective-permute-done | bytes 114720 | tf_op jit(solution)/shard_map/ppermute | solution.py:257
  18.3 1.6 collective-permute-start.5
  20.8 6.1 %collective-permute-done.5 = bf16[2,224,256]{2,1,0:T(8,128)(2,1)S(1)} collective-permute-done((bf16[2,224,256]{2,1,0:T(8,128)(2,1)S(1)}, bf16[2,224,256]{2,1,0:T(8,128)(2,1)S(1)}, u32[]{:S(2)}, u32[]{:S(2)}) %collective-permute-start.5) | collective-permute-done | bytes 229408 | tf_op jit(solution)/shard_map/ppermute | solution.py:261
  27.0 1.6 collective-permute-start.6
  28.6 6.5 %collective-permute-done.2 = bf16[2,2,224,256]{3,2,1,0:T(8,128)(2,1)S(1)} collective-permute-done((bf16[2,2,224,256]{3,2,1,0:T(8,128)(2,1)S(1)}, bf16[2,2,224,256]{3,2,1,0:T(8,128)(2,1)S(1)}, u32[]{:S(2)}, u32[]{:S(2)}) %collective-permute-start.2) | collective-permute-done | bytes 458784 | tf_op jit(solution)/shard_map/ppermute | solution.py:261
  36.9 2.2 multiply_reduce_fusion.3
  39.7 2.7 copy.97
  42.4 3.8 %maximum_select_fusion = bf16[16,2,224,256]{3,2,0,1:T(8,128)(2,1)S(1)} fusion(bf16[16,1,224,256]{3,2,0,1:T(8,128)(2,1)} %bitcast.30, bf16[16,1,224,256]{3,2,0,1:T(8,128)(2,1)S(1)} %bitcast.321, pred[]{:T(512)S(6)} %eq.56), kind=kLoop, calls=%fused_computation.5 | loop fusion | flops 5505024 | bytes 7340033 | tf_op jit(solution)/shard_map/jit(_where)/select_n | solution.py:687
  46.8 5.5 %fusion.23.maps_a = bf16[13,13,16,256]{3,2,1,0:T(8,128)(2,1)S(1)} fusion(bf16[3,3,384,256]{3,2,1,0:T(8,128)(2,1)S(1)} %bitcast.332, bf16[2,13,13,16,384]{4,3,2,1,0:T(8,128)(2,1)S(1)} %bitcast.322), kind=kOutput, calls=%fused_computation.37 | convolution fusion | flops 4307193856 | bytes 5230592 | tf_op jit(solution)/shard_map/conv_general_dilated | solution.py:701
  52.3 5.5 %fusion.22.maps_b = bf16[13,13,16,256]{3,2,1,0:T(8,128)(2,1)S(1)} fusion(bf16[3,3,384,256]{3,2,1,0:T(8,128)(2,1)S(1)} %bitcast.330, bf16[2,13,13,16,384]{4,3,2,1,0:T(8,128)(2,1)S(1)} %bitcast.323), kind=kOutput, calls=%fused_computation.36 | convolution fusion | flops 4307193856 | bytes 5230592 | tf_op jit(solution)/shard_map/conv_general_dilated | solution.py:701
  58.0 5.3 %gate_pool_mix.1 = (bf16[13,13,16,256]{3,2,1,0:T(8,128)(2,1)S(1)}, bf16[13,13,16,256]{3,2,1,0:T(8,128)(2,1)S(1)}, bf16[2,36,16,256]{3,2,1,0:T(8,128)(2,1)S(1)}, bf16[32,16,640]{2,1,0:T(8,128)(2,1)}) custom-call(bf16[13,13,16,256]{3,2,1,0:T(8,128)(2,1)S(1)} %fusion.23.maps_a, bf16[13,13,16,256]{3,2,1,0:T(8,128)(2,1)S(1)} %fusion.22.maps_b, ...), custom_call_target="tpu_custom_call" | custom-call | flops 41533440 | bytes 8306688 | tf_op jit(solution)/shard_map/gate_pool_mix/pallas_call | solution.py:398
  66.4 4.3 %all-to-all-start = ((bf16[32,16,640]{2,1,0:T(8,128)(2,1)}), bf16[32,16,640]{2,1,0:T(8,128)(2,1)S(1)}, u32[]{:S(2)}, u32[]{:S(2)}) async-start(bf16[32,16,640]{2,1,0:T(8,128)(2,1)} %get-tuple-element.38), calls=%async_computation | async-start | bytes 1310720 | tf_op jit(solution)/shard_map/all_to_all | solution.py:712
  70.7 6.6 %convert_bitcast_fusion = bf16[576,4096]{1,0:T(8,128)(2,1)} fusion(f32[1,576,4096]{2,1,0:T(8,128)} %refs_4_.1), kind=kLoop, calls=%fused_computation | loop fusion | flops 2359296 | bytes 14155776 | tf_op jit(solution)/shard_map/convert_element_type | solution.py:714
  77.4 4.3 %fusion.133 = (bf16[576,2048]{1,0:T(8,128)(2,1)}, bf16[576,2048]{1,0:T(8,128)(2,1)S(1)}) fusion(bf16[576,4096]{1,0:T(8,128)(2,1)} %convert_bitcast_fusion), kind=kLoop, calls=%fused_computation.253 | loop fusion | bytes 9437184 | tf_op jit(solution)/shard_map/slice | solution.py:717
  81.7 6.9 %all-to-all-done = bf16[32,16,640]{2,1,0:T(8,128)(2,1)S(1)} async-done(((bf16[32,16,640]{2,1,0:T(8,128)(2,1)}), bf16[32,16,640]{2,1,0:T(8,128)(2,1)S(1)}, u32[]{:S(2)}, u32[]{:S(2)}) %all-to-all-start) | async-done | bytes 655392 | tf_op jit(solution)/shard_map/all_to_all | solution.py:712
  90.3 1.4 collective-permute-start.11
  92.9 1.5 collective-permute-start.8
  94.4 9.9 %collective-permute-done.11 = bf16[2,2,32,2048]{3,2,1,0:T(8,128)(2,1)S(1)} collective-permute-done((bf16[2,2,32,2048]{3,2,1,0:T(8,128)(2,1)S(1)}, bf16[2,2,32,2048]{3,2,1,0:T(8,128)(2,1)S(1)}, u32[]{:S(2)}, u32[]{:S(2)}) %collective-permute-start.11) | collective-permute-done | bytes 524320 | tf_op jit(solution)/shard_map/ppermute | solution.py:261
  105.0 1.8 collective-permute-done.8
  115.1 1.9 collective-permute-start.14
  117.6 2.1 collective-permute-start.10
  121.2 2.2 collective-permute-done.14
  123.3 4.5 %collective-permute-done.13 = bf16[32,2048]{1,0:T(8,128)(2,1)S(1)} collective-permute-done((bf16[32,2048]{1,0:T(8,128)(2,1)S(1)}, bf16[32,2048]{1,0:T(8,128)(2,1)S(1)}, u32[]{:S(2)}, u32[]{:S(2)}) %collective-permute-start.13) | collective-permute-done | bytes 131104 | tf_op jit(solution)/shard_map/ppermute | solution.py:257
  128.2 1.5 collective-permute-start.31
  129.7 2.0 collective-permute-start.30
  137.6 1.5 collective-permute-start.25
  139.2 3.8 %collective-permute-done.30 = bf16[32,2048]{1,0:T(8,128)(2,1)S(1)} collective-permute-done((bf16[32,2048]{1,0:T(8,128)(2,1)S(1)}, bf16[32,2048]{1,0:T(8,128)(2,1)S(1)}, u32[]{:S(2)}, u32[]{:S(2)}) %collective-permute-start.30) | collective-permute-done | bytes 131104 | tf_op jit(solution)/shard_map/ppermute | solution.py:257
  144.5 2.0 collective-permute-start.23
  146.5 2.6 collective-permute-start.19
  150.0 1.7 collective-permute-done.32
  152.5 2.5 collective-permute-start.33
  155.0 1.5 collective-permute-done.22
  156.5 1.8 fusion.62
  158.4 1.8 collective-permute-start.35
  160.2 1.6 collective-permute-start.34
  162.2 3.4 %collective-permute-done.27 = bf16[32,2048]{1,0:T(8,128)(2,1)S(1)} collective-permute-done((bf16[32,2048]{1,0:T(8,128)(2,1)}, bf16[32,2048]{1,0:T(8,128)(2,1)S(1)}, u32[]{:S(2)}, u32[]{:S(2)}) %collective-permute-start.27) | collective-permute-done | bytes 131104 | tf_op jit(solution)/shard_map/ppermute | solution.py:257
  168.4 1.7 multiply_reduce_fusion.1
  170.8 5.1 %all-to-all-start.1 = ((f32[16,1,512]{2,1,0:T(1,128)}), f32[16,1,512]{2,1,0:T(1,128)S(1)}, u32[]{:S(2)}, u32[]{:S(2)}) async-start(f32[16,1,512]{2,1,0:T(1,128)} %select_n.233), calls=%async_computation.1 | async-start | bytes 65536 | tf_op jit(solution)/shard_map/all_to_all | solution.py:766
  177.0 2.1 collective-permute-start.36
  179.1 4.4 %all-to-all-done.1 = f32[16,1,512]{2,1,0:T(1,128)S(1)} async-done(((f32[16,1,512]{2,1,0:T(1,128)}), f32[16,1,512]{2,1,0:T(1,128)S(1)}, u32[]{:S(2)}, u32[]{:S(2)}) %all-to-all-start.1) | async-done | bytes 32800 | tf_op jit(solution)/shard_map/all_to_all | solution.py:766
  185.8 2.7 collective-permute-start.37
  191.0 5.4 %collective-permute-done.29 = bf16[2,2,32,2048]{3,2,1,0:T(8,128)(2,1)S(1)} collective-permute-done((bf16[2,2,32,2048]{3,2,1,0:T(8,128)(2,1)S(1)}, bf16[2,2,32,2048]{3,2,1,0:T(8,128)(2,1)S(1)}, u32[]{:S(2)}, u32[]{:S(2)}) %collective-permute-start.29) | collective-permute-done | bytes 524320 | tf_op jit(solution)/shard_map/ppermute | solution.py:261
  203.7 5.2 %all-to-all-start.2 = ((bf16[32,16,640]{2,1,0:T(8,128)(2,1)}), bf16[32,16,640]{2,1,0:T(8,128)(2,1)}, u32[]{:S(2)}, u32[]{:S(2)}) async-start(bf16[32,16,640]{2,1,0:T(8,128)(2,1)} %bitcast.318), calls=%async_computation.2 | async-start | bytes 1310720 | tf_op jit(solution)/shard_map/all_to_all | solution.py:786
  211.1 22.1 %dense_update.1 = (f32[1,576,4096]{2,1,0:T(8,128)}, f32[1,576,4096]{2,1,0:T(8,128)}, f32[1,576,4096]{2,1,0:T(8,128)}, bf16[1,576,4096]{2,1,0:T(8,128)(2,1)}, f32[1,4096]{1,0:T(1,128)S(1)}) custom-call(bf16[256,640]{1,0:T(8,128)(2,1)S(1)} %get-tuple-element.39.columns_a, bf16[256,640]{1,0:T(8,128)(2,1)S(1)} %copy-done.10, bf16[256,2048]{1,0:T(8,128)(2,1)S(1)} %bitcast.310, ...), custom_call_target="tpu_custom_call" | custom-call | flops 2684354560 | bytes 61341696 | tf_op jit(solution)/shard_map/dense_update/pallas_call | solution.py:619
  238.7 3.1 %pool_gradient.1 = (bf16[13,13,16,256]{3,2,1,0:T(8,128)(2,1)S(1)}, bf16[13,13,16,256]{3,2,1,0:T(8,128)(2,1)S(1)}, f32[6,256]{1,0:T(8,128)S(1)}) custom-call(bf16[32,16,640]{2,1,0:T(8,128)(2,1)} %all-to-all-done.2.returned, bf16[2,36,16,256]{3,2,1,0:T(8,128)(2,1)S(1)} %copy-done.8, f32[6,256]{1,0:T(8,128)S(1)} %broadcast_select_fusion.1.small, ...), custom_call_target="tpu_custom_call" | custom-call | flops 13844480 | bytes 5537792 | tf_op jit(solution)/shard_map/pool_gradient/pallas_call | solution.py:501
  242.3 7.0 %fusion.20 = bf16[3,3,384,256]{3,2,1,0:T(8,128)(2,1)S(1)} fusion(bf16[13,13,16,256]{3,2,1,0:T(8,128)(2,1)S(1)} %get-tuple-element.46, bf16[2,13,13,16,384]{4,3,2,1,0:T(8,128)(2,1)} %bitcast.324), kind=kOutput, calls=%fused_computation.34 | convolution fusion | flops 4307386368 | bytes 5230592 | tf_op jit(solution)/shard_map/conv_general_dilated | solution.py:798
  249.3 5.4 %fusion.21 = bf16[3,3,384,256]{3,2,1,0:T(8,128)(2,1)S(1)} fusion(bf16[13,13,16,256]{3,2,1,0:T(8,128)(2,1)S(1)} %get-tuple-element.45, bf16[2,13,13,16,384]{4,3,2,1,0:T(8,128)(2,1)S(1)} %bitcast.325), kind=kOutput, calls=%fused_computation.35 | convolution fusion | flops 4307386368 | bytes 5230592 | tf_op jit(solution)/shard_map/conv_general_dilated | solution.py:798
  254.8 1.5 dynamic-slice_bitcast_fusion
  256.3 1.4 pad_maximum_fusion.1
  259.9 1.8 pad_maximum_fusion.own
  264.0 1.7 collective-permute-start.39
  267.0 1.5 collective-permute-start.40
  268.6 6.8 %fusion.14 = bf16[1,13,13,16,384]{4,3,2,1,0:T(8,128)(2,1)S(1)} fusion(pred[]{:T(512)} %bitcast.99, bf16[13,13,16,256]{3,2,1,0:T(8,128)(2,1)S(1)} %copy-done.14, bf16[3,3,384,256]{3,2,1,0:T(8,128)(2,1)S(1)} %bitcast.333), kind=kOutput, calls=%fused_computation.24 | convolution fusion | flops 4308578304 | bytes 5230593 | tf_op jit(solution)/shard_map/conv_general_dilated | solution.py:842
  278.7 1.8 collective-permute-start.43
  280.5 7.1 %fusion.15 = bf16[1,13,13,16,384]{4,3,2,1,0:T(8,128)(2,1)S(1)} fusion(pred[]{:T(512)} %bitcast.101, bf16[13,13,16,256]{3,2,1,0:T(8,128)(2,1)S(1)} %get-tuple-element.46, bf16[3,3,384,256]{3,2,1,0:T(8,128)(2,1)S(1)} %bitcast.331), kind=kOutput, calls=%fused_computation.25 | convolution fusion | flops 4308578304 | bytes 5230593 | tf_op jit(solution)/shard_map/conv_general_dilated | solution.py:842
  287.8 1.5 collective-permute-start.41
  289.4 3.4 %collective-permute-start.45 = (bf16[224,256]{1,0:T(8,128)(2,1)S(1)}, bf16[224,256]{1,0:T(8,128)(2,1)S(1)}, u32[]{:S(2)}, u32[]{:S(2)}) collective-permute-start(bf16[224,256]{1,0:T(8,128)(2,1)S(1)} %get-tuple-element.196), channel_id=1, source_target_pairs={{0,24},{2,26},{4,28},{6,30},{8,16},{10,18},{12,20},{14,22},{16,8},... | collective-permute-start | bytes 344072 | tf_op jit(solution)/shard_map/ppermute | solution.py:257
  292.8 1.8 collective-permute-done.41
  294.7 1.5 collective-permute-start.42
  296.7 5.2 %copy.83 = bf16[16,2,13,13,384]{4,1,3,2,0:T(2,128)(2,1)} copy(bf16[16,2,13,13,384]{4,0,3,2,1:T(8,128)(2,1)S(1)} %maximum_bitcast_fusion) | data formatting | bytes 8306688
  (307 shorter events, 61.1 us)
Async XLA Ops:
  2.4 6.7 %collective-permute-start = (bf16[224,256]{1,0:T(8,128)(2,1)S(1)}, bf16[224,256]{1,0:T(8,128)(2,1)S(1)}, u32[]{:S(2)}, u32[]{:S(2)}) collective-permute-start(bf16[224,256]{1,0:T(8,128)(2,1)S(1)} %pad_maximum_fusion.18), channel_id=1, source_target_pairs={{0,8},{2,10},{4,12},{6,14},{8,0},{10,2},{12,4},{14,6},{16,24},{18,... | collective-permute-start | bytes 344072 | tf_op jit(solution)/shard_map/ppermute | solution.py:257
  5.5 9.0 %collective-permute-start.4 = (bf16[224,256]{1,0:T(8,128)(2,1)S(1)}, bf16[224,256]{1,0:T(8,128)(2,1)S(1)}, u32[]{:S(2)}, u32[]{:S(2)}) collective-permute-start(bf16[224,256]{1,0:T(8,128)(2,1)S(1)} %pad_maximum_fusion.18), channel_id=1, source_target_pairs={{0,24},{2,26},{4,28},{6,30},{8,16},{10,18},{12,20},{14,22},{16,8},... | collective-permute-start | bytes 344072 | tf_op jit(solution)/shard_map/ppermute | solution.py:257
  8.0 10.3 %collective-permute-start.3 = (bf16[224,256]{1,0:T(8,128)(2,1)S(1)}, bf16[224,256]{1,0:T(8,128)(2,1)S(1)}, u32[]{:S(2)}, u32[]{:S(2)}) collective-permute-start(bf16[224,256]{1,0:T(8,128)(2,1)S(1)} %pad_maximum_fusion.18), channel_id=1, source_target_pairs={{0,16},{2,18},{4,20},{6,22},{8,24},{10,26},{12,28},{14,30},{16,0},... | collective-permute-start | bytes 344072 | tf_op jit(solution)/shard_map/ppermute | solution.py:257
  9.2 11.0 %collective-permute-start.1 = (bf16[2,224,256]{2,1,0:T(8,128)(2,1)S(1)}, bf16[2,224,256]{2,1,0:T(8,128)(2,1)S(1)}, u32[]{:S(2)}, u32[]{:S(2)}) collective-permute-start(bf16[2,224,256]{2,1,0:T(8,128)(2,1)S(1)} %get-tuple-element.199), channel_id=1, source_target_pairs={{0,2},{2,0},{4,6},{6,4},{8,10},{10,8},{12,14},{14,12},{16,18},{18,... | collective-permute-start | bytes 688136 | tf_op jit(solution)/shard_map/ppermute | solution.py:261
  18.3 8.6 %collective-permute-start.5 = (bf16[2,224,256]{2,1,0:T(8,128)(2,1)S(1)}, bf16[2,224,256]{2,1,0:T(8,128)(2,1)S(1)}, u32[]{:S(2)}, u32[]{:S(2)}) collective-permute-start(bf16[2,224,256]{2,1,0:T(8,128)(2,1)S(1)} %get-tuple-element.197), channel_id=1, source_target_pairs={{0,4},{2,6},{4,0},{6,2},{8,12},{10,14},{12,8},{14,10},{16,20},{18,... | collective-permute-start | bytes 688136 | tf_op jit(solution)/shard_map/ppermute | solution.py:261
  20.2 16.3 %copy-start.56 = (s32[16]{0:T(128)S(1)}, s32[16]{0:T(128)}, u32[]{:S(2)}) copy-start(s32[16]{0:T(128)} %param.23) | copy-start | bytes 196
  20.2 14.9 %collective-permute-start.2 = (bf16[2,2,224,256]{3,2,1,0:T(8,128)(2,1)S(1)}, bf16[2,2,224,256]{3,2,1,0:T(8,128)(2,1)S(1)}, u32[]{:S(2)}, u32[]{:S(2)}) collective-permute-start(bf16[2,2,224,256]{3,2,1,0:T(8,128)(2,1)S(1)} %pad_maximum_fusion.10), channel_id=1, source_target_pairs={{0,4},{2,6},{4,0},{6,2},{8,12},{10,14},{12,8},{14,10},{16,20},{18,... | collective-permute-start | bytes 1376264 | tf_op jit(solution)/shard_map/ppermute | solution.py:261
  26.9 9.9 %copy-start.40 = (f32[2,2,2048]{2,1,0:T(2,128)S(1)}, f32[2,2,2048]{2,1,0:T(2,128)}, u32[]{:S(2)}) copy-start(f32[2,2,2048]{2,1,0:T(2,128)} %param.39) | copy-start | bytes 98308
  26.9 10.0 %copy-start.30 = (bf16[32,2,2048]{2,1,0:T(2,128)(2,1)S(1)}, bf16[32,2,2048]{2,1,0:T(2,128)(2,1)}, u32[]{:S(2)}) copy-start(bf16[32,2,2048]{2,1,0:T(2,128)(2,1)} %param.22) | copy-start | bytes 786436
  27.0 9.3 %collective-permute-start.6 = (bf16[2,2,224,256]{3,2,1,0:T(8,128)(2,1)S(1)}, bf16[2,2,224,256]{3,2,1,0:T(8,128)(2,1)S(1)}, u32[]{:S(2)}, u32[]{:S(2)}) collective-permute-start(bf16[2,2,224,256]{3,2,1,0:T(8,128)(2,1)S(1)} %pad_maximum_fusion.11), channel_id=1, source_target_pairs={{0,2},{2,0},{4,6},{6,4},{8,10},{10,8},{12,14},{14,12},{16,18},{18,... | collective-permute-start | bytes 1376264 | tf_op jit(solution)/shard_map/ppermute | solution.py:261
  36.4 6.0 %collective-permute-start.7 = (bf16[16,224,256]{2,1,0:T(8,128)(2,1)S(1)}, bf16[16,224,256]{2,1,0:T(8,128)(2,1)}, u32[]{:S(2)}, u32[]{:S(2)}) collective-permute-start(bf16[16,224,256]{2,1,0:T(8,128)(2,1)S(1)} %fusion.85), channel_id=1, source_target_pairs={{0,1},{1,0},{2,3},{3,2},{4,5},{5,4},{6,7},{7,6},{8,9},{9,8},{10,11... | collective-permute-start | bytes 5505032 | tf_op jit(solution)/shard_map/ppermute | solution.py:63
  39.2 80.6 %collective-permute-start.15 = (bf16[32,2048]{1,0:T(8,128)(2,1)}, bf16[32,2048]{1,0:T(8,128)(2,1)}, u32[]{:S(2)}, u32[]{:S(2)}) collective-permute-start(bf16[32,2048]{1,0:T(8,128)(2,1)} %get-tuple-element.145), channel_id=1, source_target_pairs={{0,1},{1,0},{2,3},{3,2},{4,5},{5,4},{6,7},{7,6},{8,9},{9,8},{10,11... | collective-permute-start | bytes 393224 | tf_op jit(solution)/shard_map/ppermute | solution.py:63
  42.4 9.9 %copy-start.15 = (bf16[16,2,13,13,384]{4,0,3,2,1:T(8,128)(2,1)}, bf16[16,2,13,13,384]{4,0,3,2,1:T(8,128)(2,1)S(1)}, u32[]{:S(2)}) copy-start(bf16[16,2,13,13,384]{4,0,3,2,1:T(8,128)(2,1)S(1)} %copy.97) | copy-start | bytes 12460036
  66.4 22.2 %all-to-all-start = ((bf16[32,16,640]{2,1,0:T(8,128)(2,1)}), bf16[32,16,640]{2,1,0:T(8,128)(2,1)S(1)}, u32[]{:S(2)}, u32[]{:S(2)}) async-start(bf16[32,16,640]{2,1,0:T(8,128)(2,1)} %get-tuple-element.38), calls=%async_computation | async-start | bytes 1310720 | tf_op jit(solution)/shard_map/all_to_all | solution.py:712
  77.4 124.8 %copy-start.11 = (s32[3]{0:T(128)}, s32[3]{0:T(128)S(1)}, u32[]{:S(2)}) copy-start(s32[3]{0:T(128)S(1)} %pad_add_fusion.place) | copy-start | bytes 40
  81.7 10.1 %copy-start.17 = (bf16[576,2048]{1,0:T(8,128)(2,1)}, bf16[576,2048]{1,0:T(8,128)(2,1)S(1)}, u32[]{:S(2)}) copy-start(bf16[576,2048]{1,0:T(8,128)(2,1)S(1)} %get-tuple-element.167) | copy-start | bytes 7077892
  89.2 21.1 %copy-start.9 = (bf16[256,640]{1,0:T(8,128)(2,1)}, bf16[256,640]{1,0:T(8,128)(2,1)S(1)}, u32[]{:S(2)}) copy-start(bf16[256,640]{1,0:T(8,128)(2,1)S(1)} %get-tuple-element.40.columns_b) | copy-start | bytes 983044
  90.3 14.0 %collective-permute-start.11 = (bf16[2,2,32,2048]{3,2,1,0:T(8,128)(2,1)S(1)}, bf16[2,2,32,2048]{3,2,1,0:T(8,128)(2,1)S(1)}, u32[]{:S(2)}, u32[]{:S(2)}) collective-permute-start(bf16[2,2,32,2048]{3,2,1,0:T(8,128)(2,1)S(1)} %bitcast.354), channel_id=1, source_target_pairs={{0,2},{2,0},{4,6},{6,4},{8,10},{10,8},{12,14},{14,12},{16,18},{18,... | collective-permute-start | bytes 1572872 | tf_op jit(solution)/shard_map/ppermute | solution.py:261
  92.9 13.9 %collective-permute-start.8 = (bf16[2,2,32,2048]{3,2,1,0:T(8,128)(2,1)S(1)}, bf16[2,2,32,2048]{3,2,1,0:T(8,128)(2,1)S(1)}, u32[]{:S(2)}, u32[]{:S(2)}) collective-permute-start(bf16[2,2,32,2048]{3,2,1,0:T(8,128)(2,1)S(1)} %bitcast.355), channel_id=1, source_target_pairs={{0,4},{2,6},{4,0},{6,2},{8,12},{10,14},{12,8},{14,10},{16,20},{18,... | collective-permute-start | bytes 1572872 | tf_op jit(solution)/shard_map/ppermute | solution.py:261
  107.5 7.6 %collective-permute-start.12 = (bf16[2,32,2048]{2,1,0:T(8,128)(2,1)S(1)}, bf16[2,32,2048]{2,1,0:T(8,128)(2,1)S(1)}, u32[]{:S(2)}, u32[]{:S(2)}) collective-permute-start(bf16[2,32,2048]{2,1,0:T(8,128)(2,1)S(1)} %fusion.64), channel_id=1, source_target_pairs={{0,4},{2,6},{4,0},{6,2},{8,12},{10,14},{12,8},{14,10},{16,20},{18,... | collective-permute-start | bytes 786440 | tf_op jit(solution)/shard_map/ppermute | solution.py:261
  108.2 9.3 %collective-permute-start.9 = (bf16[2,32,2048]{2,1,0:T(8,128)(2,1)S(1)}, bf16[2,32,2048]{2,1,0:T(8,128)(2,1)S(1)}, u32[]{:S(2)}, u32[]{:S(2)}) collective-permute-start(bf16[2,32,2048]{2,1,0:T(8,128)(2,1)S(1)} %fusion.63), channel_id=1, source_target_pairs={{0,2},{2,0},{4,6},{6,4},{8,10},{10,8},{12,14},{14,12},{16,18},{18,... | collective-permute-start | bytes 786440 | tf_op jit(solution)/shard_map/ppermute | solution.py:261
  111.5 22.0 %collective-permute-start.20 = (bf16[2,2,32,2048]{3,2,1,0:T(8,128)(2,1)S(1)}, bf16[2,2,32,2048]{3,2,1,0:T(8,128)(2,1)S(1)}, u32[]{:S(2)}, u32[]{:S(2)}) collective-permute-start(bf16[2,2,32,2048]{3,2,1,0:T(8,128)(2,1)S(1)} %bitcast.352), channel_id=1, source_target_pairs={{0,2},{2,0},{4,6},{6,4},{8,10},{10,8},{12,14},{14,12},{16,18},{18,... | collective-permute-start | bytes 1572872 | tf_op jit(solution)/shard_map/ppermute | solution.py:261
  115.1 8.2 %collective-permute-start.14 = (bf16[32,2048]{1,0:T(8,128)(2,1)S(1)}, bf16[32,2048]{1,0:T(8,128)(2,1)S(1)}, u32[]{:S(2)}, u32[]{:S(2)}) collective-permute-start(bf16[32,2048]{1,0:T(8,128)(2,1)S(1)} %get-tuple-element.194), channel_id=1, source_target_pairs={{0,24},{2,26},{4,28},{6,30},{8,16},{10,18},{12,20},{14,22},{16,8},... | collective-permute-start | bytes 393224 | tf_op jit(solution)/shard_map/ppermute | solution.py:257
  117.0 10.8 %collective-permute-start.13 = (bf16[32,2048]{1,0:T(8,128)(2,1)S(1)}, bf16[32,2048]{1,0:T(8,128)(2,1)S(1)}, u32[]{:S(2)}, u32[]{:S(2)}) collective-permute-start(bf16[32,2048]{1,0:T(8,128)(2,1)S(1)} %get-tuple-element.193), channel_id=1, source_target_pairs={{0,16},{2,18},{4,20},{6,22},{8,24},{10,26},{12,28},{14,30},{16,0},... | collective-permute-start | bytes 393224 | tf_op jit(solution)/shard_map/ppermute | solution.py:257
  117.6 10.2 %collective-permute-start.10 = (bf16[32,2048]{1,0:T(8,128)(2,1)S(1)}, bf16[32,2048]{1,0:T(8,128)(2,1)S(1)}, u32[]{:S(2)}, u32[]{:S(2)}) collective-permute-start(bf16[32,2048]{1,0:T(8,128)(2,1)S(1)} %fusion.82), channel_id=1, source_target_pairs={{0,8},{2,10},{4,12},{6,14},{8,0},{10,2},{12,4},{14,6},{16,24},{18,... | collective-permute-start | bytes 393224 | tf_op jit(solution)/shard_map/ppermute | solution.py:257
  119.8 15.2 %collective-permute-start.17 = (bf16[2,2,32,2048]{3,2,1,0:T(8,128)(2,1)S(1)}, bf16[2,2,32,2048]{3,2,1,0:T(8,128)(2,1)S(1)}, u32[]{:S(2)}, u32[]{:S(2)}) collective-permute-start(bf16[2,2,32,2048]{3,2,1,0:T(8,128)(2,1)S(1)} %bitcast.353), channel_id=1, source_target_pairs={{0,4},{2,6},{4,0},{6,2},{8,12},{10,14},{12,8},{14,10},{16,20},{18,... | collective-permute-start | bytes 1572872 | tf_op jit(solution)/shard_map/ppermute | solution.py:261
  128.1 7.7 %collective-permute-start.16 = (bf16[32,2048]{1,0:T(8,128)(2,1)S(1)}, bf16[32,2048]{1,0:T(8,128)(2,1)S(1)}, u32[]{:S(2)}, u32[]{:S(2)}) collective-permute-start(bf16[32,2048]{1,0:T(8,128)(2,1)S(1)} %get-tuple-element.164), channel_id=1, source_target_pairs={{0,8},{2,10},{4,12},{6,14},{8,0},{10,2},{12,4},{14,6},{16,24},{18,... | collective-permute-start | bytes 393224 | tf_op jit(solution)/shard_map/ppermute | solution.py:257
  128.2 11.0 %collective-permute-start.31 = (bf16[32,2048]{1,0:T(8,128)(2,1)S(1)}, bf16[32,2048]{1,0:T(8,128)(2,1)S(1)}, u32[]{:S(2)}, u32[]{:S(2)}) collective-permute-start(bf16[32,2048]{1,0:T(8,128)(2,1)S(1)} %get-tuple-element.164), channel_id=1, source_target_pairs={{0,24},{2,26},{4,28},{6,30},{8,16},{10,18},{12,20},{14,22},{16,8},... | collective-permute-start | bytes 393224 | tf_op jit(solution)/shard_map/ppermute | solution.py:257
  129.7 13.3 %collective-permute-start.30 = (bf16[32,2048]{1,0:T(8,128)(2,1)S(1)}, bf16[32,2048]{1,0:T(8,128)(2,1)S(1)}, u32[]{:S(2)}, u32[]{:S(2)}) collective-permute-start(bf16[32,2048]{1,0:T(8,128)(2,1)S(1)} %get-tuple-element.164), channel_id=1, source_target_pairs={{0,16},{2,18},{4,20},{6,22},{8,24},{10,26},{12,28},{14,30},{16,0},... | collective-permute-start | bytes 393224 | tf_op jit(solution)/shard_map/ppermute | solution.py:257
  133.7 10.7 %collective-permute-start.21 = (bf16[2,32,2048]{2,1,0:T(8,128)(2,1)S(1)}, bf16[2,32,2048]{2,1,0:T(8,128)(2,1)S(1)}, u32[]{:S(2)}, u32[]{:S(2)}) collective-permute-start(bf16[2,32,2048]{2,1,0:T(8,128)(2,1)S(1)} %fusion.66), channel_id=1, source_target_pairs={{0,4},{2,6},{4,0},{6,2},{8,12},{10,14},{12,8},{14,10},{16,20},{18,... | collective-permute-start | bytes 786440 | tf_op jit(solution)/shard_map/ppermute | solution.py:261
  135.2 11.3 %collective-permute-start.18 = (bf16[2,32,2048]{2,1,0:T(8,128)(2,1)S(1)}, bf16[2,32,2048]{2,1,0:T(8,128)(2,1)S(1)}, u32[]{:S(2)}, u32[]{:S(2)}) collective-permute-start(bf16[2,32,2048]{2,1,0:T(8,128)(2,1)S(1)} %fusion.65), channel_id=1, source_target_pairs={{0,2},{2,0},{4,6},{6,4},{8,10},{10,8},{12,14},{14,12},{16,18},{18,... | collective-permute-start | bytes 786440 | tf_op jit(solution)/shard_map/ppermute | solution.py:261
  137.6 11.5 %collective-permute-start.25 = (bf16[2,32,2048]{2,1,0:T(8,128)(2,1)S(1)}, bf16[2,32,2048]{2,1,0:T(8,128)(2,1)S(1)}, u32[]{:S(2)}, u32[]{:S(2)}) collective-permute-start(bf16[2,32,2048]{2,1,0:T(8,128)(2,1)S(1)} %get-tuple-element.188), channel_id=1, source_target_pairs={{0,2},{2,0},{4,6},{6,4},{8,10},{10,8},{12,14},{14,12},{16,18},{18,... | collective-permute-start | bytes 786440 | tf_op jit(solution)/shard_map/ppermute | solution.py:261
  143.0 8.6 %collective-permute-start.32 = (bf16[2,32,2048]{2,1,0:T(8,128)(2,1)S(1)}, bf16[2,32,2048]{2,1,0:T(8,128)(2,1)S(1)}, u32[]{:S(2)}, u32[]{:S(2)}) collective-permute-start(bf16[2,32,2048]{2,1,0:T(8,128)(2,1)S(1)} %get-tuple-element.184), channel_id=1, source_target_pairs={{0,4},{2,6},{4,0},{6,2},{8,12},{10,14},{12,8},{14,10},{16,20},{18,... | collective-permute-start | bytes 786440 | tf_op jit(solution)/shard_map/ppermute | solution.py:261
  144.5 10.6 %collective-permute-start.23 = (bf16[32,2048]{1,0:T(8,128)(2,1)S(1)}, bf16[32,2048]{1,0:T(8,128)(2,1)S(1)}, u32[]{:S(2)}, u32[]{:S(2)}) collective-permute-start(bf16[32,2048]{1,0:T(8,128)(2,1)S(1)} %get-tuple-element.192), channel_id=1, source_target_pairs={{0,24},{2,26},{4,28},{6,30},{8,16},{10,18},{12,20},{14,22},{16,8},... | collective-permute-start | bytes 393224 | tf_op jit(solution)/shard_map/ppermute | solution.py:257
  146.4 10.1 %collective-permute-start.22 = (bf16[32,2048]{1,0:T(8,128)(2,1)S(1)}, bf16[32,2048]{1,0:T(8,128)(2,1)S(1)}, u32[]{:S(2)}, u32[]{:S(2)}) collective-permute-start(bf16[32,2048]{1,0:T(8,128)(2,1)S(1)} %get-tuple-element.191), channel_id=1, source_target_pairs={{0,16},{2,18},{4,20},{6,22},{8,24},{10,26},{12,28},{14,30},{16,0},... | collective-permute-start | bytes 393224 | tf_op jit(solution)/shard_map/ppermute | solution.py:257
  146.5 10.0 %collective-permute-start.19 = (bf16[32,2048]{1,0:T(8,128)(2,1)S(1)}, bf16[32,2048]{1,0:T(8,128)(2,1)S(1)}, u32[]{:S(2)}, u32[]{:S(2)}) collective-permute-start(bf16[32,2048]{1,0:T(8,128)(2,1)S(1)} %fusion.83), channel_id=1, source_target_pairs={{0,8},{2,10},{4,12},{6,14},{8,0},{10,2},{12,4},{14,6},{16,24},{18,... | collective-permute-start | bytes 393224 | tf_op jit(solution)/shard_map/ppermute | solution.py:257
  149.2 39.3 %collective-permute-start.26 = (bf16[2,2,32,2048]{3,2,1,0:T(8,128)(2,1)S(1)}, bf16[2,2,32,2048]{3,2,1,0:T(8,128)(2,1)}, u32[]{:S(2)}, u32[]{:S(2)}) collective-permute-start(bf16[2,2,32,2048]{3,2,1,0:T(8,128)(2,1)S(1)} %pad_maximum_fusion.6), channel_id=1, source_target_pairs={{0,4},{2,6},{4,0},{6,2},{8,12},{10,14},{12,8},{14,10},{16,20},{18,... | collective-permute-start | bytes 1572872 | tf_op jit(solution)/shard_map/ppermute | solution.py:261
  151.7 14.0 %copy-start.32 = (bf16[2,32,2048]{2,1,0:T(8,128)(2,1)}, bf16[2,32,2048]{2,1,0:T(8,128)(2,1)S(1)}, u32[]{:S(2)}) copy-start(bf16[2,32,2048]{2,1,0:T(8,128)(2,1)S(1)} %collective-permute-done.32) | copy-start | bytes 786436
  152.5 15.8 %copy-start.31 = (bf16[32,2,2048]{2,1,0:T(2,128)(2,1)S(1)}, bf16[32,2,2048]{2,1,0:T(2,128)(2,1)}, u32[]{:S(2)}) copy-start(bf16[32,2,2048]{2,1,0:T(2,128)(2,1)} %param.22) | copy-start | bytes 786436
  152.5 37.1 %collective-permute-start.33 = (bf16[2,2,32,2048]{3,2,1,0:T(8,128)(2,1)}, bf16[2,2,32,2048]{3,2,1,0:T(8,128)(2,1)}, u32[]{:S(2)}, u32[]{:S(2)}) collective-permute-start(bf16[2,2,32,2048]{3,2,1,0:T(8,128)(2,1)} %pad_maximum_fusion.8), channel_id=1, source_target_pairs={{0,2},{2,0},{4,6},{6,4},{8,10},{10,8},{12,14},{14,12},{16,18},{18,... | collective-permute-start | bytes 1572872 | tf_op jit(solution)/shard_map/ppermute | solution.py:261
  158.4 7.3 %collective-permute-start.27 = (bf16[32,2048]{1,0:T(8,128)(2,1)}, bf16[32,2048]{1,0:T(8,128)(2,1)S(1)}, u32[]{:S(2)}, u32[]{:S(2)}) collective-permute-start(bf16[32,2048]{1,0:T(8,128)(2,1)} %fusion.62), channel_id=1, source_target_pairs={{0,8},{2,10},{4,12},{6,14},{8,0},{10,2},{12,4},{14,6},{16,24},{18,... | collective-permute-start | bytes 393224 | tf_op jit(solution)/shard_map/ppermute | solution.py:257
  158.4 17.6 %collective-permute-start.35 = (bf16[32,2048]{1,0:T(8,128)(2,1)}, bf16[32,2048]{1,0:T(8,128)(2,1)}, u32[]{:S(2)}, u32[]{:S(2)}) collective-permute-start(bf16[32,2048]{1,0:T(8,128)(2,1)} %fusion.62), channel_id=1, source_target_pairs={{0,24},{2,26},{4,28},{6,30},{8,16},{10,18},{12,20},{14,22},{16,8},... | collective-permute-start | bytes 393224 | tf_op jit(solution)/shard_map/ppermute | solution.py:257
  160.2 15.7 %collective-permute-start.34 = (bf16[32,2048]{1,0:T(8,128)(2,1)}, bf16[32,2048]{1,0:T(8,128)(2,1)}, u32[]{:S(2)}, u32[]{:S(2)}) collective-permute-start(bf16[32,2048]{1,0:T(8,128)(2,1)} %fusion.62), channel_id=1, source_target_pairs={{0,16},{2,18},{4,20},{6,22},{8,24},{10,26},{12,28},{14,30},{16,0},... | collective-permute-start | bytes 393224 | tf_op jit(solution)/shard_map/ppermute | solution.py:257
  165.6 1.3 collective-permute-start.24
  166.6 19.1 %copy-start.21 = (bf16[1,2,32,2048]{3,2,1,0:T(8,128)(2,1)}, bf16[1,2,32,2048]{3,2,1,0:T(8,128)(2,1)S(1)}, u32[]{:S(2)}) copy-start(bf16[1,2,32,2048]{3,2,1,0:T(8,128)(2,1)S(1)} %get-tuple-element.189) | copy-start | bytes 786436
  167.0 16.6 %collective-permute-start.28 = (bf16[2,32,2048]{2,1,0:T(8,128)(2,1)S(1)}, bf16[2,32,2048]{2,1,0:T(8,128)(2,1)S(1)}, u32[]{:S(2)}, u32[]{:S(2)}) collective-permute-start(bf16[2,32,2048]{2,1,0:T(8,128)(2,1)S(1)} %get-tuple-element.190), channel_id=1, source_target_pairs={{0,2},{2,0},{4,6},{6,4},{8,10},{10,8},{12,14},{14,12},{16,18},{18,... | collective-permute-start | bytes 786440 | tf_op jit(solution)/shard_map/ppermute | solution.py:261
  170.8 12.6 %all-to-all-start.1 = ((f32[16,1,512]{2,1,0:T(1,128)}), f32[16,1,512]{2,1,0:T(1,128)S(1)}, u32[]{:S(2)}, u32[]{:S(2)}) async-start(f32[16,1,512]{2,1,0:T(1,128)} %select_n.233), calls=%async_computation.1 | async-start | bytes 65536 | tf_op jit(solution)/shard_map/all_to_all | solution.py:766
  177.0 12.7 %copy-start.23 = (bf16[1,2,32,2048]{3,2,1,0:T(8,128)(2,1)}, bf16[1,2,32,2048]{3,2,1,0:T(8,128)(2,1)S(1)}, u32[]{:S(2)}) copy-start(bf16[1,2,32,2048]{3,2,1,0:T(8,128)(2,1)S(1)} %get-tuple-element.185) | copy-start | bytes 786436
  177.0 8.7 %collective-permute-start.36 = (bf16[2,32,2048]{2,1,0:T(8,128)(2,1)S(1)}, bf16[2,32,2048]{2,1,0:T(8,128)(2,1)S(1)}, u32[]{:S(2)}, u32[]{:S(2)}) collective-permute-start(bf16[2,32,2048]{2,1,0:T(8,128)(2,1)S(1)} %get-tuple-element.186), channel_id=1, source_target_pairs={{0,4},{2,6},{4,0},{6,2},{8,12},{10,14},{12,8},{14,10},{16,20},{18,... | collective-permute-start | bytes 786440 | tf_op jit(solution)/shard_map/ppermute | solution.py:261
  183.7 12.7 %collective-permute-start.29 = (bf16[2,2,32,2048]{3,2,1,0:T(8,128)(2,1)S(1)}, bf16[2,2,32,2048]{3,2,1,0:T(8,128)(2,1)S(1)}, u32[]{:S(2)}, u32[]{:S(2)}) collective-permute-start(bf16[2,2,32,2048]{3,2,1,0:T(8,128)(2,1)S(1)} %pad_maximum_fusion.7), channel_id=1, source_target_pairs={{0,4},{2,6},{4,0},{6,2},{8,12},{10,14},{12,8},{14,10},{16,20},{18,... | collective-permute-start | bytes 1572872 | tf_op jit(solution)/shard_map/ppermute | solution.py:261
  185.8 12.2 %collective-permute-start.37 = (bf16[2,2,32,2048]{3,2,1,0:T(8,128)(2,1)S(1)}, bf16[2,2,32,2048]{3,2,1,0:T(8,128)(2,1)S(1)}, u32[]{:S(2)}, u32[]{:S(2)}) collective-permute-start(bf16[2,2,32,2048]{3,2,1,0:T(8,128)(2,1)S(1)} %pad_maximum_fusion.9), channel_id=1, source_target_pairs={{0,2},{2,0},{4,6},{6,4},{8,10},{10,8},{12,14},{14,12},{16,18},{18,... | collective-permute-start | bytes 1572872 | tf_op jit(solution)/shard_map/ppermute | solution.py:261
  188.4 8.0 %copy-start.22 = (bf16[1,2,32,2048]{3,2,1,0:T(8,128)(2,1)S(1)}, bf16[1,2,32,2048]{3,2,1,0:T(8,128)(2,1)}, u32[]{:S(2)}) copy-start(bf16[1,2,32,2048]{3,2,1,0:T(8,128)(2,1)} %copy-done.21) | copy-start | bytes 786436
  188.4 8.0 %copy-start.35 = (bf16[2,32,2048]{2,1,0:T(8,128)(2,1)S(1)}, bf16[2,32,2048]{2,1,0:T(8,128)(2,1)}, u32[]{:S(2)}) copy-start(bf16[2,32,2048]{2,1,0:T(8,128)(2,1)} %copy-done.34) | copy-start | bytes 786436
  203.7 31.3 %all-to-all-start.2 = ((bf16[32,16,640]{2,1,0:T(8,128)(2,1)}), bf16[32,16,640]{2,1,0:T(8,128)(2,1)}, u32[]{:S(2)}, u32[]{:S(2)}) async-start(bf16[32,16,640]{2,1,0:T(8,128)(2,1)} %bitcast.318), calls=%async_computation.2 | async-start | bytes 1310720 | tf_op jit(solution)/shard_map/all_to_all | solution.py:786
  211.1 31.0 %copy-start.48 = (f32[8]{0:T(128)}, f32[8]{0:T(128)S(1)}, u32[]{:S(2)}) copy-start(f32[8]{0:T(128)S(1)} %multiply_add_fusion.5) | copy-start | bytes 100
  241.9 7.5 %copy-start.13 = (bf16[13,13,16,256]{3,2,1,0:T(8,128)(2,1)}, bf16[13,13,16,256]{3,2,1,0:T(8,128)(2,1)S(1)}, u32[]{:S(2)}) copy-start(bf16[13,13,16,256]{3,2,1,0:T(8,128)(2,1)S(1)} %get-tuple-element.45) | copy-start | bytes 4153348
  257.7 4.8 %collective-permute-start.38 = (bf16[16,224,256]{2,1,0:T(8,128)(2,1)}, bf16[16,224,256]{2,1,0:T(8,128)(2,1)S(1)}, u32[]{:S(2)}, u32[]{:S(2)}) collective-permute-start(bf16[16,224,256]{2,1,0:T(8,128)(2,1)} %pad_maximum_fusion.1), channel_id=1, source_target_pairs={{0,1},{1,0},{2,3},{3,2},{4,5},{5,4},{6,7},{7,6},{8,9},{9,8},{10,11... | collective-permute-start | bytes 5505032 | tf_op jit(solution)/shard_map/ppermute | solution.py:63
  264.0 12.8 %collective-permute-start.39 = (bf16[2,2,224,256]{3,2,1,0:T(8,128)(2,1)S(1)}, bf16[2,2,224,256]{3,2,1,0:T(8,128)(2,1)S(1)}, u32[]{:S(2)}, u32[]{:S(2)}) collective-permute-start(bf16[2,2,224,256]{3,2,1,0:T(8,128)(2,1)S(1)} %slice.348), channel_id=1, source_target_pairs={{0,2},{2,0},{4,6},{6,4},{8,10},{10,8},{12,14},{14,12},{16,18},{18,... | collective-permute-start | bytes 1376264 | tf_op jit(solution)/shard_map/ppermute | solution.py:261
  267.0 20.6 %collective-permute-start.40 = (bf16[2,2,224,256]{3,2,1,0:T(8,128)(2,1)S(1)}, bf16[2,2,224,256]{3,2,1,0:T(8,128)(2,1)S(1)}, u32[]{:S(2)}, u32[]{:S(2)}) collective-permute-start(bf16[2,2,224,256]{3,2,1,0:T(8,128)(2,1)S(1)} %slice.351), channel_id=1, source_target_pairs={{0,4},{2,6},{4,0},{6,2},{8,12},{10,14},{12,8},{14,10},{16,20},{18,... | collective-permute-start | bytes 1376264 | tf_op jit(solution)/shard_map/ppermute | solution.py:261
  278.7 10.6 %collective-permute-start.43 = (bf16[2,224,256]{2,1,0:T(8,128)(2,1)S(1)}, bf16[2,224,256]{2,1,0:T(8,128)(2,1)S(1)}, u32[]{:S(2)}, u32[]{:S(2)}) collective-permute-start(bf16[2,224,256]{2,1,0:T(8,128)(2,1)S(1)} %fusion.77), channel_id=1, source_target_pairs={{0,4},{2,6},{4,0},{6,2},{8,12},{10,14},{12,8},{14,10},{16,20},{18,... | collective-permute-start | bytes 688136 | tf_op jit(solution)/shard_map/ppermute | solution.py:261
  287.8 6.9 %collective-permute-start.41 = (bf16[2,224,256]{2,1,0:T(8,128)(2,1)S(1)}, bf16[2,224,256]{2,1,0:T(8,128)(2,1)S(1)}, u32[]{:S(2)}, u32[]{:S(2)}) collective-permute-start(bf16[2,224,256]{2,1,0:T(8,128)(2,1)S(1)} %fusion.76), channel_id=1, source_target_pairs={{0,2},{2,0},{4,6},{6,4},{8,10},{10,8},{12,14},{14,12},{16,18},{18,... | collective-permute-start | bytes 688136 | tf_op jit(solution)/shard_map/ppermute | solution.py:261
  289.4 12.6 %collective-permute-start.45 = (bf16[224,256]{1,0:T(8,128)(2,1)S(1)}, bf16[224,256]{1,0:T(8,128)(2,1)S(1)}, u32[]{:S(2)}, u32[]{:S(2)}) collective-permute-start(bf16[224,256]{1,0:T(8,128)(2,1)S(1)} %get-tuple-element.196), channel_id=1, source_target_pairs={{0,24},{2,26},{4,28},{6,30},{8,16},{10,18},{12,20},{14,22},{16,8},... | collective-permute-start | bytes 344072 | tf_op jit(solution)/shard_map/ppermute | solution.py:257
  292.8 9.2 %collective-permute-start.44 = (bf16[224,256]{1,0:T(8,128)(2,1)S(1)}, bf16[224,256]{1,0:T(8,128)(2,1)S(1)}, u32[]{:S(2)}, u32[]{:S(2)}) collective-permute-start(bf16[224,256]{1,0:T(8,128)(2,1)S(1)} %get-tuple-element.195), channel_id=1, source_target_pairs={{0,16},{2,18},{4,20},{6,22},{8,24},{10,26},{12,28},{14,30},{16,0},... | collective-permute-start | bytes 344072 | tf_op jit(solution)/shard_map/ppermute | solution.py:257
  294.7 7.3 %collective-permute-start.42 = (bf16[224,256]{1,0:T(8,128)(2,1)S(1)}, bf16[224,256]{1,0:T(8,128)(2,1)S(1)}, u32[]{:S(2)}, u32[]{:S(2)}) collective-permute-start(bf16[224,256]{1,0:T(8,128)(2,1)S(1)} %fusion.84), channel_id=1, source_target_pairs={{0,8},{2,10},{4,12},{6,14},{8,0},{10,2},{12,4},{14,6},{16,24},{18,... | collective-permute-start | bytes 344072 | tf_op jit(solution)/shard_map/ppermute | solution.py:257
  (42 other events, 128.6 us)
